TPU v7x, 32 devices: a whole 2x2x4 slice. The times are simulated.
32 devices in a mesh: ctx: 8 (over y, x, core), tp: 4 (over z).
Axes of the slice: x: 2, y: 2, z: 4, core: 2. Of those that a mesh axis runs over, the one named last changes fastest.
Arguments:
- queries: bfloat16 [2048, 2048], P('ctx', 'tp'), may hold values from -6 to 6
- keys_copied: bfloat16 [2048, 512], P('ctx', 'tp'), may hold values from -6 to 6, as said below
- values_copied: bfloat16 [2048, 512], P('ctx', 'tp'), may hold values from -6 to 6, as said below
- attention_output_saved: bfloat16 [2048, 2048], P('ctx', 'tp'), may hold values from -6 to 6
- log_norm: float32 [16, 2048], P('tp', 'ctx'), as said below
- block_output_gradient: bfloat16 [2048, 8192], P(('ctx', 'tp')), may hold values from -6 to 6
- w_out: bfloat16 [2048, 8192], P('tp'), may hold values from -0.125 to 0.125
- adapter_down_factor: bfloat16 [2048, 64], P('tp'), may hold values from -0.125 to 0.125
- adapter_up: bfloat16 [64, 8192], replicated, may hold values from -0.0625 to 0.0625
Outputs:
- grad_query: bfloat16 [2048, 2048], P('ctx', 'tp')
- grad_keys: bfloat16 [2048, 512], P('ctx', 'tp')
- grad_values: bfloat16 [2048, 512], P('ctx', 'tp')
- down_factor_gradient: float32 [2048, 64], P('tp')
- up_factor_gradient: bfloat16 [64, 8192], replicated
Inputs may be any that keep to these rules, and one draw needn't show every extreme that they name: log_norm[h, r] minus the natural logarithm of (1 + pos(r)) lies between 0 and 1.5. `keys_copied`: for every g below 2, the 128 columns from 2 * g * 128 equal the 128 columns that follow them. `values_copied`: for every g below 2, the 128 columns from 2 * g * 128 equal the 128 columns that follow them.
All inputs are finite; a program needn't handle non-finite values.
Results may differ from a plain program's by a relative error of at most 0.022.
Values may be sent and summed in bfloat16 or wider, within the bound.
A program may use at most 64 MiB of HBM per device.

v0:
```python
import jax
import jax.numpy as jnp
from jax import lax
from jax.sharding import PartitionSpec as P

adapter_scale_factor = 2.0


def passed_along(x, axis, by):
    size = lax.axis_size(axis)
    return lax.ppermute(x, axis, [(i, (i + by) % size) for i in range(size)])


def partner(x, axis, distance):
    return lax.ppermute(x, axis, [(i, i ^ 1 << distance) for i in range(lax.axis_size(axis))])


def folded_positions(device, device_count, row_count):
    half_rows = row_count // 2
    offset_rows = jnp.arange(row_count, dtype=jnp.int32)
    early_pos = device * half_rows + offset_rows
    late_pos = (2 * device_count - 1 - device) * half_rows + offset_rows - half_rows
    return jnp.where(offset_rows < half_rows, early_pos, late_pos)


def local(
    queries,
    keys_copied,
    values_copied,
    attention_output_saved,
    log_norm,
    block_output_gradient,
    w_out,
    adapter_down_factor,
    adapter_up,
):
    ctx_count = lax.axis_size("ctx")
    ctx_index = lax.axis_index("ctx")
    row_count = queries.shape[0]
    head_count = log_norm.shape[0]
    proj_rows = w_out.shape[0]
    head_dim = proj_rows // head_count
    softmax_scale = head_dim ** (-0.5)
    contract_last = (((1,), (1,)), ((), ()))
    contract_first = (((0,), (0,)), ((), ()))
    frozen_weight_gradient = lax.dot_general(
        lax.all_gather(block_output_gradient, "tp", axis=0, tiled=True),
        w_out,
        contract_last,
        preferred_element_type=jnp.float32,
    )
    up_rows = lax.dot_general(
        block_output_gradient, adapter_up, contract_last, preferred_element_type=jnp.float32
    ).astype(jnp.bfloat16)
    adapter_cotangent_rows = lax.all_gather(up_rows, "tp", axis=0, tiled=True)
    adapter_input_gradient = lax.dot_general(
        adapter_cotangent_rows,
        adapter_down_factor,
        contract_last,
        preferred_element_type=jnp.float32,
    )
    attention_output_gradient = (
        frozen_weight_gradient + adapter_scale_factor * adapter_input_gradient
    ).astype(jnp.bfloat16)
    mixed_rows = lax.psum_scatter(
        jnp.dot(attention_output_saved, adapter_down_factor, preferred_element_type=jnp.float32),
        "tp",
        scatter_dimension=0,
        tiled=True,
    ).astype(jnp.bfloat16)
    partial_up_gradient = adapter_scale_factor * lax.dot_general(
        mixed_rows, block_output_gradient, contract_first, preferred_element_type=jnp.float32
    )
    partial_down_gradient = adapter_scale_factor * lax.dot_general(
        attention_output_saved,
        adapter_cotangent_rows,
        contract_first,
        preferred_element_type=jnp.float32,
    )
    down_factor_gradient = lax.psum(partial_down_gradient.astype(jnp.bfloat16), "ctx").astype(
        jnp.float32
    )
    up_factor_gradient = lax.psum(partial_up_gradient, ("ctx", "tp"))
    up_factor_gradient = up_factor_gradient.astype(jnp.bfloat16)
    query_heads = queries.reshape(row_count, head_count, head_dim)
    grad_heads = attention_output_gradient.reshape(row_count, head_count, head_dim)
    output_heads = attention_output_saved.reshape(row_count, head_count, head_dim)
    row_delta = jnp.sum(grad_heads.astype(jnp.float32) * output_heads.astype(jnp.float32), axis=2).T
    query_pos = folded_positions(ctx_index, ctx_count, row_count)

    def visit(keys_block, values_block, source):
        key_pos = folded_positions(source, ctx_count, row_count)
        visible = query_pos[:, None] >= key_pos[None, :]
        scores = (
            jnp.einsum("qhd,kd->hqk", query_heads, keys_block, preferred_element_type=jnp.float32)
            * softmax_scale
        )
        attn_prob = jnp.where(visible[None], jnp.exp(scores - log_norm[:, :, None]), 0.0)
        probs_low = attn_prob.astype(jnp.bfloat16)
        value_grad = jnp.einsum(
            "hqk,qhd->kd", probs_low, grad_heads, preferred_element_type=jnp.float32
        )
        prob_grad = jnp.einsum(
            "qhd,kd->hqk", grad_heads, values_block, preferred_element_type=jnp.float32
        )
        score_grad = (attn_prob * (prob_grad - row_delta[:, :, None])).astype(jnp.bfloat16)
        query_grad = (
            jnp.einsum("hqk,kd->qhd", score_grad, keys_block, preferred_element_type=jnp.float32)
            * softmax_scale
        )
        key_grad = (
            jnp.einsum("hqk,qhd->kd", score_grad, query_heads, preferred_element_type=jnp.float32)
            * softmax_scale
        )
        return (query_grad, key_grad, value_grad)

    query_acc, key_own, value_own = visit(keys_copied, values_copied, ctx_index)

    def cycle_step(step_index, loop_state):
        stream, query_sum = loop_state
        keys_block, values_block, key_acc, value_acc = stream
        keys_block, values_block = passed_along((keys_block, values_block), "ctx", 1)
        key_acc, value_acc = passed_along((key_acc, value_acc), "ctx", 1)
        query_grad, key_grad, value_grad = visit(
            keys_block, values_block, (ctx_index - step_index) % ctx_count
        )
        return (
            (keys_block, values_block, key_acc + key_grad, value_acc + value_grad),
            query_sum + query_grad,
        )

    stream, query_acc = lax.fori_loop(
        1, ctx_count, cycle_step, ((keys_copied, values_copied, key_own, value_own), query_acc)
    )
    key_total, value_total = (
        passed_along(stream[2].astype(jnp.bfloat16), "ctx", 1).astype(jnp.float32),
        passed_along(stream[3].astype(jnp.bfloat16), "ctx", 1).astype(jnp.float32),
    )
    key_recv, value_recv = (
        partner(key_total.astype(jnp.bfloat16), "tp", 0).astype(key_total.dtype),
        partner(value_total.astype(jnp.bfloat16), "tp", 0).astype(value_total.dtype),
    )
    grad_keys = (key_total + key_recv).astype(jnp.bfloat16)
    grad_values = (value_total + value_recv).astype(jnp.bfloat16)
    grad_query = query_acc.reshape(row_count, proj_rows).astype(jnp.bfloat16)
    return (grad_query, grad_keys, grad_values, down_factor_gradient, up_factor_gradient)


def solution(mesh):
    placed = (
        P("ctx", "tp"),
        P("ctx", "tp"),
        P("ctx", "tp"),
        P("ctx", "tp"),
        P("tp", "ctx"),
        P(("ctx", "tp"), None),
        P("tp", None),
        P("tp", None),
        P(),
    )
    return jax.shard_map(
        local,
        mesh=mesh,
        in_specs=placed,
        out_specs=(P("ctx", "tp"), P("ctx", "tp"), P("ctx", "tp"), P("tp", None), P()),
        check_vma=False,
    )
```

profile of v0, /device:TPU:0, one launch (start us, length us, event | category | flops | bytes accessed | tf_op | source)
XLA Modules:
  0.0 282.9 jit_solution(184795790075945778)
XLA Ops:
  12.2 14.9 %all_gather.7 = bf16[256,64]{1,0:T(8,128)(2,1)S(1)} all-gather(bf16[64,64]{1,0:T(8,128)(2,1)S(1)} %convolution_convert_fusion), channel_id=1, replica_groups=mesh['ctx'=8,'tp'=4] {'tp'}, dimensions={0}, use_global_device_ids=true | all-gather | bytes 40960 | tf_op jit(solution)/shard_map/all_gather | solution.py:55
  27.1 1.8 fusion.31
  29.0 1.8 fusion.38
  34.7 48.0 %all-reduce.3.cloned.1.call-done = bf16[512,64]{0,1:T(8,128)(2,1)} async-done(((bf16[512,64]{0,1:T(8,128)(2,1)}), bf16[512,64]{0,1:T(8,128)(2,1)}) %all-reduce.3.cloned.1.call-update) | async-done | bytes 65552 | tf_op jit(solution)/shard_map/psum | solution.py:80
  84.2 2.6 convolution_multiply_fusion.2
  86.8 45.6 %all-gather.2.cloned.1.call-done = bf16[256,8192]{1,0:T(8,128)(2,1)} async-done(((bf16[64,8192]{1,0:T(8,128)(2,1)}), bf16[256,8192]{1,0:T(8,128)(2,1)}) %all-gather.2.cloned.1.call-update) | async-done | bytes 4194320 | tf_op jit(solution)/shard_map/all_gather | solution.py:47
  132.3 7.0 %fusion.37 = f32[256,512]{1,0:T(8,128)S(1)} fusion(bf16[256,8192]{1,0:T(8,128)(2,1)} %all-gather.2.cloned.1.call-done, bf16[512,8192]{1,0:T(8,128)(2,1)} %param.17), kind=kOutput, calls=%fused_computation.61 | convolution fusion | flops 2147483648 | bytes 13107200 | tf_op jit(solution)/shard_map/dot_general | solution.py:46
  144.2 60.7 %while.24 = (s32[]{:T(128)}, bf16[256,128]{1,0:T(8,128)(2,1)}, bf16[256,128]{1,0:T(8,128)(2,1)}, f32[256,128]{1,0:T(8,128)S(1)}, f32[256,128]{1,0:T(8,128)S(1)},...) while((s32[]{:T(128)}, bf16[256,128]{1,0:T(8,128)(2,1)}, ...), condition=%wide.region_2.0_spmd.clone, body=%wide.region_1.0_spmd.clone.sunk | while | flops 337807872 | bytes 9515514 | solution.py:132
  147.6 2.2 collective-permute-done
  153.7 2.4 collective-permute-start.2
  156.2 2.2 collective-permute-done
  162.3 2.4 collective-permute-start.2
  164.9 2.2 collective-permute-done
  171.0 2.4 collective-permute-start.2
  173.5 2.2 collective-permute-done
  179.6 2.4 collective-permute-start.2
  182.2 2.2 collective-permute-done
  188.3 2.4 collective-permute-start.2
  190.9 2.2 collective-permute-done
  197.0 2.4 collective-permute-start.2
  199.5 2.2 collective-permute-done
  204.9 61.0 %all-reduce.4 = bf16[64,8192]{1,0:T(8,128)(2,1)} all-reduce(f32[64,8192]{1,0:T(8,128)} %convolution_multiply_fusion.2), channel_id=1, replica_groups=mesh['ctx'=8,'tp'=4] {'ctx','tp'}, use_global_device_ids=true, to_apply=%region_5.6 | all-reduce | flops 524288 | bytes 3145728 | tf_op jit(solution)/shard_map/psum | solution.py:83
  267.5 3.1 %collective-permute-done.4 = bf16[256,128]{1,0:T(8,128)(2,1)S(1)} collective-permute-done((bf16[256,128]{1,0:T(8,128)(2,1)S(1)}, bf16[256,128]{1,0:T(8,128)(2,1)S(1)}, u32[]{:S(2)}, u32[]{:S(2)}) %collective-permute-start.4) | collective-permute-done | bytes 65568 | tf_op jit(solution)/shard_map/ppermute | solution.py:11
  271.9 2.9 %collective-permute-done.5 = bf16[256,128]{1,0:T(8,128)(2,1)S(1)} collective-permute-done((bf16[256,128]{1,0:T(8,128)(2,1)S(1)}, bf16[256,128]{1,0:T(8,128)(2,1)S(1)}, u32[]{:S(2)}, u32[]{:S(2)}) %collective-permute-start.5) | collective-permute-done | bytes 65568 | tf_op jit(solution)/shard_map/ppermute | solution.py:15
  (168 shorter events, 48.1 us)
Async XLA Ops:
  8.1 74.6 %all-reduce.3.cloned.1.call-start = ((), (), s32[]{:S(2)}) async-start(), calls=%async_computation.2 | async-start | bytes 131072 | tf_op jit(solution)/shard_map/psum | solution.py:80
  28.9 55.3 %reduce-scatter.2.cloned.1.call-start = ((), (), s32[]{:S(2)}) async-start(), calls=%async_computation.3 | async-start | bytes 163840 | tf_op jit(solution)/shard_map/reduce_scatter | solution.py:65
  30.8 101.5 %all-gather.2.cloned.1.call-start = ((), (), s32[]{:S(2)}) async-start(), calls=%async_computation.1 | async-start | bytes 5242880 | tf_op jit(solution)/shard_map/all_gather | solution.py:47
  144.2 5.9 %collective-permute-start.1 = (bf16[256,128]{1,0:T(8,128)(2,1)}, bf16[256,128]{1,0:T(8,128)(2,1)S(1)}, u32[]{:S(2)}, u32[]{:S(2)}) collective-permute-start(bf16[256,128]{1,0:T(8,128)(2,1)} %get-tuple-element.493), channel_id=1, source_target_pairs={{0,4},{4,8},{8,12},{12,16},{16,20},{20,24},{24,28},{28,0},{1,5},{5... | collective-permute-start | bytes 196616 | tf_op jit(solution)/shard_map/while/body/eval_jaxpr/ppermute | solution.py:11
  145.8 6.2 %collective-permute-start.3 = (f32[256,128]{1,0:T(8,128)S(1)}, f32[256,128]{1,0:T(8,128)S(1)}, u32[]{:S(2)}, u32[]{:S(2)}) collective-permute-start(f32[256,128]{1,0:T(8,128)S(1)} %get-tuple-element.495), channel_id=1, source_target_pairs={{0,4},{4,8},{8,12},{12,16},{16,20},{20,24},{24,28},{28,0},{1,5},{5... | collective-permute-start | bytes 393224 | tf_op jit(solution)/shard_map/while/body/eval_jaxpr/ppermute | solution.py:11
  145.9 6.6 %collective-permute-start.2 = (f32[256,128]{1,0:T(8,128)S(1)}, f32[256,128]{1,0:T(8,128)S(1)}, u32[]{:S(2)}, u32[]{:S(2)}) collective-permute-start(f32[256,128]{1,0:T(8,128)S(1)} %get-tuple-element.494), channel_id=1, source_target_pairs={{0,4},{4,8},{8,12},{12,16},{16,20},{20,24},{24,28},{28,0},{1,5},{5... | collective-permute-start | bytes 393224 | tf_op jit(solution)/shard_map/while/body/eval_jaxpr/ppermute | solution.py:11
  152.8 5.9 %collective-permute-start.1 = (bf16[256,128]{1,0:T(8,128)(2,1)}, bf16[256,128]{1,0:T(8,128)(2,1)S(1)}, u32[]{:S(2)}, u32[]{:S(2)}) collective-permute-start(bf16[256,128]{1,0:T(8,128)(2,1)} %get-tuple-element.493), channel_id=1, source_target_pairs={{0,4},{4,8},{8,12},{12,16},{16,20},{20,24},{24,28},{28,0},{1,5},{5... | collective-permute-start | bytes 196616 | tf_op jit(solution)/shard_map/while/body/eval_jaxpr/ppermute | solution.py:11
  153.6 7.1 %collective-permute-start.3 = (f32[256,128]{1,0:T(8,128)S(1)}, f32[256,128]{1,0:T(8,128)S(1)}, u32[]{:S(2)}, u32[]{:S(2)}) collective-permute-start(f32[256,128]{1,0:T(8,128)S(1)} %get-tuple-element.495), channel_id=1, source_target_pairs={{0,4},{4,8},{8,12},{12,16},{16,20},{20,24},{24,28},{28,0},{1,5},{5... | collective-permute-start | bytes 393224 | tf_op jit(solution)/shard_map/while/body/eval_jaxpr/ppermute | solution.py:11
  153.7 7.5 %collective-permute-start.2 = (f32[256,128]{1,0:T(8,128)S(1)}, f32[256,128]{1,0:T(8,128)S(1)}, u32[]{:S(2)}, u32[]{:S(2)}) collective-permute-start(f32[256,128]{1,0:T(8,128)S(1)} %get-tuple-element.494), channel_id=1, source_target_pairs={{0,4},{4,8},{8,12},{12,16},{16,20},{20,24},{24,28},{28,0},{1,5},{5... | collective-permute-start | bytes 393224 | tf_op jit(solution)/shard_map/while/body/eval_jaxpr/ppermute | solution.py:11
  161.5 5.9 %collective-permute-start.1 = (bf16[256,128]{1,0:T(8,128)(2,1)}, bf16[256,128]{1,0:T(8,128)(2,1)S(1)}, u32[]{:S(2)}, u32[]{:S(2)}) collective-permute-start(bf16[256,128]{1,0:T(8,128)(2,1)} %get-tuple-element.493), channel_id=1, source_target_pairs={{0,4},{4,8},{8,12},{12,16},{16,20},{20,24},{24,28},{28,0},{1,5},{5... | collective-permute-start | bytes 196616 | tf_op jit(solution)/shard_map/while/body/eval_jaxpr/ppermute | solution.py:11
  162.2 7.1 %collective-permute-start.3 = (f32[256,128]{1,0:T(8,128)S(1)}, f32[256,128]{1,0:T(8,128)S(1)}, u32[]{:S(2)}, u32[]{:S(2)}) collective-permute-start(f32[256,128]{1,0:T(8,128)S(1)} %get-tuple-element.495), channel_id=1, source_target_pairs={{0,4},{4,8},{8,12},{12,16},{16,20},{20,24},{24,28},{28,0},{1,5},{5... | collective-permute-start | bytes 393224 | tf_op jit(solution)/shard_map/while/body/eval_jaxpr/ppermute | solution.py:11
  162.3 7.6 %collective-permute-start.2 = (f32[256,128]{1,0:T(8,128)S(1)}, f32[256,128]{1,0:T(8,128)S(1)}, u32[]{:S(2)}, u32[]{:S(2)}) collective-permute-start(f32[256,128]{1,0:T(8,128)S(1)} %get-tuple-element.494), channel_id=1, source_target_pairs={{0,4},{4,8},{8,12},{12,16},{16,20},{20,24},{24,28},{28,0},{1,5},{5... | collective-permute-start | bytes 393224 | tf_op jit(solution)/shard_map/while/body/eval_jaxpr/ppermute | solution.py:11
  170.9 7.1 %collective-permute-start.3 = (f32[256,128]{1,0:T(8,128)S(1)}, f32[256,128]{1,0:T(8,128)S(1)}, u32[]{:S(2)}, u32[]{:S(2)}) collective-permute-start(f32[256,128]{1,0:T(8,128)S(1)} %get-tuple-element.495), channel_id=1, source_target_pairs={{0,4},{4,8},{8,12},{12,16},{16,20},{20,24},{24,28},{28,0},{1,5},{5... | collective-permute-start | bytes 393224 | tf_op jit(solution)/shard_map/while/body/eval_jaxpr/ppermute | solution.py:11
  171.0 7.6 %collective-permute-start.2 = (f32[256,128]{1,0:T(8,128)S(1)}, f32[256,128]{1,0:T(8,128)S(1)}, u32[]{:S(2)}, u32[]{:S(2)}) collective-permute-start(f32[256,128]{1,0:T(8,128)S(1)} %get-tuple-element.494), channel_id=1, source_target_pairs={{0,4},{4,8},{8,12},{12,16},{16,20},{20,24},{24,28},{28,0},{1,5},{5... | collective-permute-start | bytes 393224 | tf_op jit(solution)/shard_map/while/body/eval_jaxpr/ppermute | solution.py:11
  178.8 5.9 %collective-permute-start.1 = (bf16[256,128]{1,0:T(8,128)(2,1)}, bf16[256,128]{1,0:T(8,128)(2,1)S(1)}, u32[]{:S(2)}, u32[]{:S(2)}) collective-permute-start(bf16[256,128]{1,0:T(8,128)(2,1)} %get-tuple-element.493), channel_id=1, source_target_pairs={{0,4},{4,8},{8,12},{12,16},{16,20},{20,24},{24,28},{28,0},{1,5},{5... | collective-permute-start | bytes 196616 | tf_op jit(solution)/shard_map/while/body/eval_jaxpr/ppermute | solution.py:11
  179.6 7.1 %collective-permute-start.3 = (f32[256,128]{1,0:T(8,128)S(1)}, f32[256,128]{1,0:T(8,128)S(1)}, u32[]{:S(2)}, u32[]{:S(2)}) collective-permute-start(f32[256,128]{1,0:T(8,128)S(1)} %get-tuple-element.495), channel_id=1, source_target_pairs={{0,4},{4,8},{8,12},{12,16},{16,20},{20,24},{24,28},{28,0},{1,5},{5... | collective-permute-start | bytes 393224 | tf_op jit(solution)/shard_map/while/body/eval_jaxpr/ppermute | solution.py:11
  179.6 7.6 %collective-permute-start.2 = (f32[256,128]{1,0:T(8,128)S(1)}, f32[256,128]{1,0:T(8,128)S(1)}, u32[]{:S(2)}, u32[]{:S(2)}) collective-permute-start(f32[256,128]{1,0:T(8,128)S(1)} %get-tuple-element.494), channel_id=1, source_target_pairs={{0,4},{4,8},{8,12},{12,16},{16,20},{20,24},{24,28},{28,0},{1,5},{5... | collective-permute-start | bytes 393224 | tf_op jit(solution)/shard_map/while/body/eval_jaxpr/ppermute | solution.py:11
  187.5 5.9 %collective-permute-start.1 = (bf16[256,128]{1,0:T(8,128)(2,1)}, bf16[256,128]{1,0:T(8,128)(2,1)S(1)}, u32[]{:S(2)}, u32[]{:S(2)}) collective-permute-start(bf16[256,128]{1,0:T(8,128)(2,1)} %get-tuple-element.493), channel_id=1, source_target_pairs={{0,4},{4,8},{8,12},{12,16},{16,20},{20,24},{24,28},{28,0},{1,5},{5... | collective-permute-start | bytes 196616 | tf_op jit(solution)/shard_map/while/body/eval_jaxpr/ppermute | solution.py:11
  188.2 7.1 %collective-permute-start.3 = (f32[256,128]{1,0:T(8,128)S(1)}, f32[256,128]{1,0:T(8,128)S(1)}, u32[]{:S(2)}, u32[]{:S(2)}) collective-permute-start(f32[256,128]{1,0:T(8,128)S(1)} %get-tuple-element.495), channel_id=1, source_target_pairs={{0,4},{4,8},{8,12},{12,16},{16,20},{20,24},{24,28},{28,0},{1,5},{5... | collective-permute-start | bytes 393224 | tf_op jit(solution)/shard_map/while/body/eval_jaxpr/ppermute | solution.py:11
  188.3 7.6 %collective-permute-start.2 = (f32[256,128]{1,0:T(8,128)S(1)}, f32[256,128]{1,0:T(8,128)S(1)}, u32[]{:S(2)}, u32[]{:S(2)}) collective-permute-start(f32[256,128]{1,0:T(8,128)S(1)} %get-tuple-element.494), channel_id=1, source_target_pairs={{0,4},{4,8},{8,12},{12,16},{16,20},{20,24},{24,28},{28,0},{1,5},{5... | collective-permute-start | bytes 393224 | tf_op jit(solution)/shard_map/while/body/eval_jaxpr/ppermute | solution.py:11
  196.2 5.9 %collective-permute-start.1 = (bf16[256,128]{1,0:T(8,128)(2,1)}, bf16[256,128]{1,0:T(8,128)(2,1)S(1)}, u32[]{:S(2)}, u32[]{:S(2)}) collective-permute-start(bf16[256,128]{1,0:T(8,128)(2,1)} %get-tuple-element.493), channel_id=1, source_target_pairs={{0,4},{4,8},{8,12},{12,16},{16,20},{20,24},{24,28},{28,0},{1,5},{5... | collective-permute-start | bytes 196616 | tf_op jit(solution)/shard_map/while/body/eval_jaxpr/ppermute | solution.py:11
  196.9 7.1 %collective-permute-start.3 = (f32[256,128]{1,0:T(8,128)S(1)}, f32[256,128]{1,0:T(8,128)S(1)}, u32[]{:S(2)}, u32[]{:S(2)}) collective-permute-start(f32[256,128]{1,0:T(8,128)S(1)} %get-tuple-element.495), channel_id=1, source_target_pairs={{0,4},{4,8},{8,12},{12,16},{16,20},{20,24},{24,28},{28,0},{1,5},{5... | collective-permute-start | bytes 393224 | tf_op jit(solution)/shard_map/while/body/eval_jaxpr/ppermute | solution.py:11
  197.0 7.6 %collective-permute-start.2 = (f32[256,128]{1,0:T(8,128)S(1)}, f32[256,128]{1,0:T(8,128)S(1)}, u32[]{:S(2)}, u32[]{:S(2)}) collective-permute-start(f32[256,128]{1,0:T(8,128)S(1)} %get-tuple-element.494), channel_id=1, source_target_pairs={{0,4},{4,8},{8,12},{12,16},{16,20},{20,24},{24,28},{28,0},{1,5},{5... | collective-permute-start | bytes 393224 | tf_op jit(solution)/shard_map/while/body/eval_jaxpr/ppermute | solution.py:11
  204.8 61.1 %collective-permute-start.6 = (bf16[256,128]{1,0:T(8,128)(2,1)S(1)}, bf16[256,128]{1,0:T(8,128)(2,1)S(1)}, u32[]{:S(2)}, u32[]{:S(2)}) collective-permute-start(bf16[256,128]{1,0:T(8,128)(2,1)S(1)} %convert_element_type.101), channel_id=1, source_target_pairs={{0,4},{4,8},{8,12},{12,16},{16,20},{20,24},{24,28},{28,0},{1,5},{5... | collective-permute-start | bytes 196616 | tf_op jit(solution)/shard_map/ppermute | solution.py:11
  (20 other events, 342.1 us)
Sparse Core Ops, SparseCore 0:
  29.1 53.6 all-reduce.2
Sparse Core Ops, SparseCore 1:
  31.6 20.3 reduce-scatter.1
  53.5 78.8 all-gather.1
where the time goes:
time: 284 us; the launch traced here: 283 us
  waiting for transfers between devices  117 us (41%)
  blocking collectives  75.9 us (27%)
  matrix products  30.4 us (11%)
  starting transfers between devices  24.4 us (9%)
  between operations  15.7 us (6%)
  local copies, waits for them, and re-layouts  13.3 us (5%)
  other arithmetic  5.86 us (2%)
    psum x1, blocking collectives, local(): up_factor_gradient = lax.psum(partial_up_gradient, ('ctx', 'tp'))  61 us
    psum x1, waiting for transfers between devices, local(): lax.psum(partial_down_gradient.astype(jnp.bfloat16), 'ctx')  48 us
    all_gather x1, waiting for transfers between devices, local(): lax.all_gather(block_output_gradient, 'tp', axis=0, tiled=True)  45.6 us
    ppermute x30, starting transfers between devices, passed_along(): return lax.ppermute(x, axis, [(i, (i + by) % size) for i in range(size)])  22.8 us
    ppermute x30, waiting for transfers between devices, passed_along(): return lax.ppermute(x, axis, [(i, (i + by) % size) for i in range(size)])  19.7 us
    all_gather x1, blocking collectives, local(): adapter_cotangent_rows = lax.all_gather(up_rows, 'tp', axis=0, tiled=True)  14.9 us
    while x14, local copies, waits for them, and re-layouts  8.83 us
    dot_general x1, matrix products, local(): lax.dot_general(lax.all_gather(block_output_gradient, 'tp', axis=0, tiled...  7.01 us
  transfers between devices with their start and end apart: 35, of which 18 were waited for; matrix products, arithmetic and copies ran while one was open for 10% of the time, Pallas kernels for 0%

commit v1 on v0

v1 whole, which is shorter than its diff:
```python
import functools

import jax
import jax.numpy as jnp
from jax import lax
from jax.experimental import pallas as pl
from jax.experimental.pallas import tpu as pltpu
from jax.sharding import PartitionSpec as P

adapter_scale_factor = 2.0
MESH = pl.DeviceIdType.MESH
F32 = jnp.float32
BF16 = jnp.bfloat16
NT = (((1,), (1,)), ((), ()))
TN = (((0,), (0,)), ((), ()))
CHUNKS = 4


def dot(a, b, dims=(((1,), (0,)), ((), ()))):
    return lax.dot_general(a, b, dims, preferred_element_type=F32)


def kernel(
    ctx_n, tp_n, heads,
    q_ref, k_ref, v_ref, ao_ref, ln_ref, g_hbm, w_hbm, down_ref, up_ref,
    dq_out, dk_out, dv_out, down_out, up_out,
    gath, w, dacc, down_pad,
    cot, mix_send, mix_recv,
    u_send, u_recv, uz, u_all,
    d_recv, kv, probs, q_st, do_st, ln_st, delta_st, dq_st,
    dkv_acc, dkv_send, dkv_recv, pair_buf,
    loc_sem, gr_s, gr_r, gl_s, gl_r,
    kv_s, kv_r, cot_s, cot_r, mix_s, mix_r, u_s, u_r, uz_s, uz_r, ua_s, ua_r,
    d_s, d_r, dkv_s, dkv_r, pair_s, pair_r,
):
    c = lax.axis_index("ctx")
    z = lax.axis_index("tp")
    rows = q_ref.shape[0]
    half = rows // 2
    blk = rows // tp_n
    width = g_hbm.shape[1]
    cw = width // CHUNKS
    uw = width // ctx_n
    rank = down_ref.shape[1]
    hd = q_ref.shape[1] // heads
    scale = hd ** (-0.5)
    cells = 2 * ctx_n

    w_copies = [
        pltpu.make_async_copy(
            w_hbm.at[:, pl.ds(i * cw, cw)], w.at[i], loc_sem.at[CHUNKS + i]
        )
        for i in range(CHUNKS)
    ]
    g_copies = [
        pltpu.make_async_copy(g_hbm.at[:, pl.ds(i * cw, cw)], gath.at[z, i], loc_sem.at[i])
        for i in range(CHUNKS)
    ]
    for cp in g_copies:
        cp.start()
    for cp in w_copies:
        cp.start()

    barrier = pltpu.get_barrier_semaphore()
    for k in range(1, ctx_n):
        pl.semaphore_signal(
            barrier, inc=1, device_id={"ctx": lax.rem(c + k, ctx_n), "tp": z}, device_id_type=MESH
        )
    for k in range(1, tp_n):
        pl.semaphore_signal(
            barrier, inc=1, device_id={"ctx": c, "tp": lax.rem(z + k, tp_n)}, device_id_type=MESH
        )
    pl.semaphore_wait(barrier, ctx_n - 1 + tp_n - 1)

    def ctx_copy(k, src, dst, s, r):
        return pltpu.make_async_remote_copy(
            src_ref=src, dst_ref=dst, send_sem=s.at[k], recv_sem=r.at[k],
            device_id={"ctx": lax.rem(c + k, ctx_n), "tp": z}, device_id_type=MESH,
        )

    def tp_copy(k, src, dst, s, r):
        return pltpu.make_async_remote_copy(
            src_ref=src, dst_ref=dst, send_sem=s.at[k], recv_sem=r.at[k],
            device_id={"ctx": c, "tp": lax.rem(z + k, tp_n)}, device_id_type=MESH,
        )

    def right_copy(s, i):
        return pltpu.make_async_remote_copy(
            src_ref=gath.at[z - s, i], dst_ref=gath.at[z - s, i],
            send_sem=gr_s.at[s, i], recv_sem=gr_r.at[s, i],
            device_id={"ctx": c, "tp": z + 1}, device_id_type=MESH,
        )

    def left_copy(s, i):
        return pltpu.make_async_remote_copy(
            src_ref=gath.at[z + s, i], dst_ref=gath.at[z + s, i],
            send_sem=gl_s.at[s, i], recv_sem=gl_r.at[s, i],
            device_id={"ctx": c, "tp": z - 1}, device_id_type=MESH,
        )

    def sends_right(s):
        return jnp.logical_and(z - s >= 0, z + 1 < tp_n)

    def sends_left(s):
        return jnp.logical_and(z + s < tp_n, z - 1 >= 0)

    for i in range(CHUNKS):
        g_copies[i].wait()

        @pl.when(sends_right(0))
        def _(i=i):
            right_copy(0, i).start()

        @pl.when(sends_left(0))
        def _(i=i):
            left_copy(0, i).start()

    kv[c, 0] = k_ref[...]
    kv[c, 1] = v_ref[...]
    kv_copies = [ctx_copy(k, kv.at[c], kv.at[c], kv_s, kv_r) for k in range(1, ctx_n)]
    for cp in kv_copies:
        cp.start()

    down_pad[...] = jnp.zeros_like(down_pad)
    down_pad[:, :rank] = down_ref[...]
    cot_own = jnp.zeros((blk, rank), F32)
    for i in range(CHUNKS):
        cot_own += dot(gath[z, i], up_ref[:, i * cw : (i + 1) * cw], NT)
    cot[z] = jnp.zeros((blk, cot.shape[2]), BF16)
    cot[z, :, :rank] = cot_own.astype(BF16)
    cot_copies = [tp_copy(k, cot.at[z], cot.at[z], cot_s, cot_r) for k in range(1, tp_n)]
    for cp in cot_copies:
        cp.start()
    mix_send[...] = dot(ao_ref[...], down_pad[...]).reshape(mix_send.shape)
    mix_copies = [
        tp_copy(k, mix_send.at[lax.rem(z + k, tp_n)], mix_recv.at[z], mix_s, mix_r)
        for k in range(1, tp_n)
    ]
    for cp in mix_copies:
        cp.start()
    mix_recv[z] = mix_send[z]

    for part in range(2):
        for h in range(heads):
            q_st[part, h * half : (h + 1) * half, :] = q_ref[
                part * half : (part + 1) * half, h * hd : (h + 1) * hd
            ]
            ln_st[part, :, h * half : (h + 1) * half] = ln_ref[
                h : h + 1, part * half : (part + 1) * half
            ]
    dq_st[...] = jnp.zeros_like(dq_st)
    dkv_acc[...] = jnp.zeros_like(dkv_acc)

    for cp in w_copies:
        cp.wait()

    def project(b, i):
        dacc[b] += dot(gath[b, i], w[i], NT)

    dacc[...] = jnp.zeros_like(dacc)
    for i in range(CHUNKS):
        project(z, i)

    def place(pair):
        early = pair <= c
        cell = jnp.where(early, pair, pair - c - 1)
        part = jnp.where(early, 0, 1)
        late_cell = cell >= ctx_n
        dev = jnp.where(late_cell, cells - 1 - cell, cell)
        start = pl.multiple_of(jnp.where(late_cell, half, 0), half)
        return early, cell, part, dev, start

    ctx_up_copies = [
        ctx_copy(k, u_send.at[lax.rem(c + k, ctx_n)], u_recv.at[c], u_s, u_r)
        for k in range(1, ctx_n)
    ]
    d_copies = [ctx_copy(k, d_recv.at[c], d_recv.at[c], d_s, d_r) for k in range(1, ctx_n)]
    uz_copies = [tp_copy(k, uz.at[z], uz.at[z], uz_s, uz_r) for k in range(1, tp_n)]
    ua_copies = [ctx_copy(k, u_all.at[c], u_all.at[c], ua_s, ua_r) for k in range(1, ctx_n)]

    def first_parts():
        for cp in mix_copies:
            cp.wait_recv()
        mixed = mix_recv[0]
        for t in range(1, tp_n):
            mixed += mix_recv[t]
        mixed = mixed.astype(BF16)
        for j in range(ctx_n):
            i, off = (j * uw) // cw, (j * uw) % cw
            part = dot(mixed, gath[z, i, :, off : off + uw], TN)
            u_send[j] = (adapter_scale_factor * part[:rank]).astype(BF16)
        for cp in ctx_up_copies:
            cp.start()
        u_recv[c] = u_send[c]
        for cp in cot_copies:
            cp.wait_recv()
        cot_rows = cot[...].reshape(rows, cot.shape[2])
        part = dot(cot_rows, ao_ref[...], TN)
        d_recv[c] = (adapter_scale_factor * part[:rank]).astype(BF16)
        for cp in d_copies:
            cp.start()

    def probabilities():
        for cp in kv_copies:
            cp.wait_recv()

        def body(pair, _):
            early, cell, part, dev, start = place(pair)
            keys = kv[dev, 0, pl.ds(start, half), :]
            scores = dot(keys, q_st[part], NT) * scale
            q_cell = jnp.where(early, c, cells - 1 - c)
            shape = (half, half)
            key_pos = cell * half + lax.broadcasted_iota(jnp.int32, shape, 0)
            q_pos = q_cell * half + lax.broadcasted_iota(jnp.int32, shape, 1)
            seen = q_pos >= key_pos
            for h in range(heads):
                cols = slice(h * half, (h + 1) * half)
                p = jnp.exp(scores[:, cols] - ln_st[part, :, cols])
                probs[pair, :, cols] = jnp.where(seen, p, 0.0)
            return 0

        lax.fori_loop(0, cells + 1, body, 0)

    def second_parts():
        for cp in ctx_up_copies:
            cp.wait_recv()
        total = u_recv[0].astype(F32)
        for j in range(1, ctx_n):
            total += u_recv[j].astype(F32)
        uz[z] = total.astype(BF16)
        for cp in uz_copies:
            cp.start()
        for cp in d_copies:
            cp.wait_recv()
        total = d_recv[0].astype(F32)
        for j in range(1, ctx_n):
            total += d_recv[j].astype(F32)
        down_out[...] = total

    def third_parts():
        for cp in uz_copies:
            cp.wait_recv()
        total = uz[0].astype(F32)
        for t in range(1, tp_n):
            total += uz[t].astype(F32)
        u_all[c] = total.astype(BF16)
        for cp in ua_copies:
            cp.start()

    for s in range(tp_n - 1):
        from_left = z - 1 - s >= 0
        from_right = z + 1 + s < tp_n
        for i in range(CHUNKS):
            @pl.when(from_left)
            def _(s=s, i=i):
                right_copy(s, i).wait_recv()

                @pl.when(z + 1 < tp_n)
                def _():
                    pltpu.make_async_remote_copy(
                        src_ref=gath.at[z - 1 - s, i], dst_ref=gath.at[z - 1 - s, i],
                        send_sem=gr_s.at[s + 1, i], recv_sem=gr_r.at[s + 1, i],
                        device_id={"ctx": c, "tp": z + 1}, device_id_type=MESH,
                    ).start()

                project(z - 1 - s, i)

            @pl.when(from_right)
            def _(s=s, i=i):
                left_copy(s, i).wait_recv()

                @pl.when(z - 1 >= 0)
                def _():
                    pltpu.make_async_remote_copy(
                        src_ref=gath.at[z + 1 + s, i], dst_ref=gath.at[z + 1 + s, i],
                        send_sem=gl_s.at[s + 1, i], recv_sem=gl_r.at[s + 1, i],
                        device_id={"ctx": c, "tp": z - 1}, device_id_type=MESH,
                    ).start()

                project(z + 1 + s, i)

            if s == 0 and i == 0:
                first_parts()
            if s == 0 and i == 2:
                probabilities()
            if s == 1 and i == 0:
                second_parts()
            if s == 1 and i == 2:
                third_parts()

    cot_rows = cot[...].reshape(rows, cot.shape[2])
    d_attn = dacc[...].reshape(rows, dacc.shape[2]) + adapter_scale_factor * dot(
        cot_rows, down_pad[...], NT
    )
    d_attn = d_attn.astype(BF16)
    for part in range(2):
        for h in range(heads):
            r0, c0 = part * half, h * hd
            block = d_attn[r0 : r0 + half, c0 : c0 + hd]
            do_st[part, h * half : (h + 1) * half, :] = block
            prod = block.astype(F32) * ao_ref[r0 : r0 + half, c0 : c0 + hd].astype(F32)
            delta_st[part, :, h * half : (h + 1) * half] = jnp.sum(prod.T, axis=0, keepdims=True)

    def backward(pair, _):
        early, cell, part, dev, start = place(pair)
        keys = kv[dev, 0, pl.ds(start, half), :]
        values = kv[dev, 1, pl.ds(start, half), :]
        p = probs[pair]
        grads = do_st[part]
        prob_grad = dot(values, grads, NT)
        score_grad = (p * (prob_grad - delta_st[part])).astype(BF16)
        dkv_acc[dev, 1, pl.ds(start, half), :] += dot(p.astype(BF16), grads)
        dkv_acc[dev, 0, pl.ds(start, half), :] += dot(score_grad, q_st[part])
        dq_st[part] += dot(score_grad, keys, TN)
        return 0

    lax.fori_loop(0, cells + 1, backward, 0)

    dkv_copies = [
        ctx_copy(k, dkv_send.at[lax.rem(c + k, ctx_n)], dkv_recv.at[c], dkv_s, dkv_r)
        for k in range(1, ctx_n)
    ]
    for k in list(range(1, ctx_n)):
        j = lax.rem(c + k, ctx_n)
        dkv_send[j, 0] = (dkv_acc[j, 0] * scale).astype(BF16)
        dkv_send[j, 1] = dkv_acc[j, 1].astype(BF16)
        dkv_copies[k - 1].start()
    dkv_recv[c, 0] = (dkv_acc[c, 0] * scale).astype(BF16)
    dkv_recv[c, 1] = dkv_acc[c, 1].astype(BF16)

    for part in range(2):
        for h in range(heads):
            dq_out[part * half : (part + 1) * half, h * hd : (h + 1) * hd] = (
                dq_st[part, h * half : (h + 1) * half, :] * scale
            ).astype(BF16)
    for cp in ua_copies:
        cp.wait_recv()
    for j in range(ctx_n):
        up_out[:, j * uw : (j + 1) * uw] = u_all[j]

    for cp in dkv_copies:
        cp.wait_recv()
    total = dkv_recv[0].astype(F32)
    for j in range(1, ctx_n):
        total += dkv_recv[j].astype(F32)
    pair_buf[0] = total.astype(BF16)
    other = z + 1 - 2 * lax.rem(z, 2)
    pair_copy = pltpu.make_async_remote_copy(
        src_ref=pair_buf.at[0], dst_ref=pair_buf.at[1], send_sem=pair_s, recv_sem=pair_r,
        device_id={"ctx": c, "tp": other}, device_id_type=MESH,
    )
    pair_copy.start()
    pair_copy.wait_recv()
    sums = pair_buf[0].astype(F32) + pair_buf[1].astype(F32)
    dk_out[...] = sums[0].astype(BF16)
    dv_out[...] = sums[1].astype(BF16)

    for group in (
        kv_copies, cot_copies, mix_copies, ctx_up_copies, d_copies, uz_copies, ua_copies, dkv_copies
    ):
        for cp in group:
            cp.wait_send()
    pair_copy.wait_send()
    for s in range(tp_n - 1):
        for i in range(CHUNKS):
            @pl.when(sends_right(s))
            def _(s=s, i=i):
                right_copy(s, i).wait_send()

            @pl.when(sends_left(s))
            def _(s=s, i=i):
                left_copy(s, i).wait_send()


def local(q, k, v, ao, ln, g, w, down, up):
    ctx_n = lax.axis_size("ctx")
    tp_n = lax.axis_size("tp")
    rows, q_cols = q.shape
    heads = ln.shape[0]
    hd = q_cols // heads
    half = rows // 2
    blk = rows // tp_n
    width = g.shape[1]
    cw = width // CHUNKS
    uw = width // ctx_n
    proj = w.shape[0]
    rank = down.shape[1]
    lanes = max(128, rank)
    pairs = 2 * ctx_n + 1
    vmem = pl.BlockSpec(memory_space=pltpu.VMEM)
    hbm = pl.BlockSpec(memory_space=pl.ANY)
    V = pltpu.VMEM
    DMA = pltpu.SemaphoreType.DMA
    scratch = [
        V((tp_n, CHUNKS, blk, cw), BF16),
        V((CHUNKS, proj, cw), BF16),
        V((tp_n, blk, proj), F32),
        V((proj, lanes), BF16),
        V((tp_n, blk, lanes), BF16),
        V((tp_n, blk, lanes), F32),
        V((tp_n, blk, lanes), F32),
        V((ctx_n, rank, uw), BF16),
        V((ctx_n, rank, uw), BF16),
        V((tp_n, rank, uw), BF16),
        V((ctx_n, rank, uw), BF16),
        V((ctx_n, rank, proj), BF16),
        V((ctx_n, 2, rows, hd), BF16),
        V((pairs, half, heads * half), F32),
        V((2, heads * half, hd), BF16),
        V((2, heads * half, hd), BF16),
        V((2, 1, heads * half), F32),
        V((2, 1, heads * half), F32),
        V((2, heads * half, hd), F32),
        V((ctx_n, 2, rows, hd), F32),
        V((ctx_n, 2, rows, hd), BF16),
        V((ctx_n, 2, rows, hd), BF16),
        V((2, 2, rows, hd), BF16),
        DMA((2 * CHUNKS,)),
    ]
    scratch += [DMA((tp_n, CHUNKS))] * 4
    scratch += [DMA((ctx_n,))] * 2 + [DMA((tp_n,))] * 4 + [DMA((ctx_n,))] * 2
    scratch += [DMA((tp_n,))] * 2 + [DMA((ctx_n,))] * 6 + [DMA, DMA]
    dq, dk, dv, dd, du = pl.pallas_call(
        functools.partial(kernel, ctx_n, tp_n, heads),
        out_shape=(
            jax.ShapeDtypeStruct(q.shape, BF16),
            jax.ShapeDtypeStruct(k.shape, BF16),
            jax.ShapeDtypeStruct(v.shape, BF16),
            jax.ShapeDtypeStruct((rank, proj), F32),
            jax.ShapeDtypeStruct(up.shape, BF16),
        ),
        in_specs=[vmem] * 5 + [hbm] * 2 + [vmem] * 2,
        out_specs=(vmem,) * 5,
        scratch_shapes=scratch,
        compiler_params=pltpu.CompilerParams(
            collective_id=0, has_side_effects=True, vmem_limit_bytes=60 * 2**20
        ),
        cost_estimate=pl.CostEstimate(
            flops=5 * 10**9, bytes_accessed=16 * 2**20, transcendentals=2**21
        ),
    )(q, k, v, ao, ln, g, w, down, up)
    return dq, dk, dv, dd.T, du


def solution(mesh):
    placed = (
        P("ctx", "tp"),
        P("ctx", "tp"),
        P("ctx", "tp"),
        P("ctx", "tp"),
        P("tp", "ctx"),
        P(("ctx", "tp"), None),
        P("tp", None),
        P("tp", None),
        P(),
    )
    return jax.shard_map(
        local,
        mesh=mesh,
        in_specs=placed,
        out_specs=(P("ctx", "tp"), P("ctx", "tp"), P("ctx", "tp"), P("tp", None), P()),
        check_vma=False,
    )
```

time: 284 us -> 123 us (0.43)
  waiting for transfers between devices: 117 us -> 0 us
  Pallas kernels: 0 us -> 112 us
  blocking collectives: 75.9 us -> 0 us
  matrix products: 30.4 us -> 0 us
  starting transfers between devices: 24.4 us -> 0 us
  between operations: 15.7 us -> 0.64 us
  other arithmetic: 5.86 us -> 0 us
  local copies, waits for them, and re-layouts: 13.3 us -> 10 us
    pallas_call x0 -> x1, Pallas kernels: none -> 112 us  [local(): pl.pallas_call(functools.partial(kernel, ctx_n, tp_n, heads), out_shape=(...]
    psum x1 -> x0, blocking collectives: 61 us -> none  [local(): up_factor_gradient = lax.psum(partial_up_gradient, ('ctx', 'tp'))]
    psum x1 -> x0, waiting for transfers between devices: 48 us -> none  [local(): lax.psum(partial_down_gradient.astype(jnp.bfloat16), 'ctx')]
    all_gather x1 -> x0, waiting for transfers between devices: 45.6 us -> none  [local(): lax.all_gather(block_output_gradient, 'tp', axis=0, tiled=True)]
    dot_general x46 -> x0, matrix products: 30.4 us -> none  [the longest x1 7.01 us: local(): lax.dot_general(lax.all_gather(block_output_gradient, 'tp', axis=0, tiled...]
    ppermute x32 -> x0, starting transfers between devices: 24.3 us -> none  [the longest x30 22.8 us: passed_along(): return lax.ppermute(x, axis, [(i, (i + by) % size) for i in range(size)])]
    ppermute x32 -> x0, waiting for transfers between devices: 22.6 us -> none  [the longest x30 19.7 us: passed_along(): return lax.ppermute(x, axis, [(i, (i + by) % size) for i in range(size)])]
    all_gather x1 -> x0, blocking collectives: 14.9 us -> none  [local(): adapter_cotangent_rows = lax.all_gather(up_rows, 'tp', axis=0, tiled=True)]
  transfers between devices with their start and end apart: 35 -> 0, of which waited for: 18 -> 0; matrix products, arithmetic and copies ran while one was open for 10% -> 0% of each run, Pallas kernels for 0% -> 0%
where the time goes in v1:
time: 123 us
  Pallas kernels  112 us (91%)
  local copies, waits for them, and re-layouts  10 us (8%)
    pallas_call x1, Pallas kernels, local(): pl.pallas_call(functools.partial(kernel, ctx_n, tp_n, heads), out_shape=(...  112 us
    unnamed x6, local copies, waits for them, and re-layouts  10 us

profile of v1, /device:TPU:0, one launch (start us, length us, event | category | flops | bytes accessed | tf_op | source)
XLA Modules:
  0.0 122.9 jit_solution(4461252536832181592)
XLA Ops:
  0.6 1.6 %copy.14.down_ref = bf16[512,64]{1,0:T(8,128)(2,1)} copy(bf16[512,64]{0,1:T(8,128)(2,1)} %param.16) | data formatting | bytes 131072 | tf_op args[7]
  2.2 112.2 %shard_map.128 = (bf16[256,512]{1,0:T(8,128)(2,1)}, bf16[256,128]{1,0:T(8,128)(2,1)}, bf16[256,128]{1,0:T(8,128)(2,1)}, f32[64,512]{1,0:T(8,128)}, bf16[64,8192]{1,0:T(8,128)(2,1)}) custom-call(bf16[256,512]{1,0:T(8,128)(2,1)} %q_ref.1, bf16[256,128]{1,0:T(8,128)(2,1)} %k_ref.1, bf16[256,128]{1,0:T(8,128)(2,1)} %v_ref.1, bf16[256,512]{1,0:T(8,128)(2,1)} %ao_ref.1, ...), custom_call_target="tpu_custom_call" | custom-call | flops 5000000000 | bytes 16777216 | tf_op jit(solution)/shard_map/pallas_call | solution.py:423
  114.5 1.7 %copy.20 = bf16[256,512]{1,0:T(8,128)(2,1)} copy(bf16[256,512]{1,0:T(8,128)(2,1)} %get-tuple-element.20) | data formatting | bytes 524288
  116.2 1.5 %copy.21 = bf16[256,128]{1,0:T(8,128)(2,1)} copy(bf16[256,128]{1,0:T(8,128)(2,1)} %get-tuple-element.21) | data formatting | bytes 131072
  117.6 1.5 %copy.22 = bf16[256,128]{1,0:T(8,128)(2,1)} copy(bf16[256,128]{1,0:T(8,128)(2,1)} %get-tuple-element.22) | data formatting | bytes 131072
  119.1 1.6 %copy.23 = f32[512,64]{0,1:T(8,128)} copy(f32[512,64]{0,1:T(8,128)} %bitcast.1) | data formatting | bytes 262144
  120.7 2.3 %copy.24 = bf16[64,8192]{1,0:T(8,128)(2,1)} copy(bf16[64,8192]{1,0:T(8,128)(2,1)} %get-tuple-element.24) | data formatting | bytes 2097152

commit v2 on v1

--- a/solution.py
+++ b/solution.py
@@ -13,7 +13,9 @@
 BF16 = jnp.bfloat16
 NT = (((1,), (1,)), ((), ()))
 TN = (((0,), (0,)), ((), ()))
-CHUNKS = 4
+CHUNKS = 8
+MOVED = 3
+KEPT = CHUNKS - MOVED
 
 
 def dot(a, b, dims=(((1,), (0,)), ((), ()))):
@@ -26,12 +28,12 @@
     dq_out, dk_out, dv_out, down_out, up_out,
     gath, w, dacc, down_pad,
     cot, mix_send, mix_recv,
-    u_send, u_recv, uz, u_all,
+    u_send, u_recv, u_sum, uz, uc, u_all, wx, px_send, px_recv,
     d_recv, kv, probs, q_st, do_st, ln_st, delta_st, dq_st,
     dkv_acc, dkv_send, dkv_recv, pair_buf,
     loc_sem, gr_s, gr_r, gl_s, gl_r,
-    kv_s, kv_r, cot_s, cot_r, mix_s, mix_r, u_s, u_r, uz_s, uz_r, ua_s, ua_r,
-    d_s, d_r, dkv_s, dkv_r, pair_s, pair_r,
+    kv_s, kv_r, cot_s, cot_r, mix_s, mix_r, u_s, u_r, uz_s, uz_r, uc_s, uc_r, ua_s, ua_r,
+    d_s, d_r, dkv_s, dkv_r, px_s, px_r, wa_s, wa_r, wf_s, wf_r, we_s, we_r, pair_s, pair_r,
 ):
     c = lax.axis_index("ctx")
     z = lax.axis_index("tp")
@@ -41,7 +43,7 @@
     width = g_hbm.shape[1]
     cw = width // CHUNKS
     uw = width // ctx_n
-    rank = down_ref.shape[1]
+    rank = down_ref.shape[0]
     hd = q_ref.shape[1] // heads
     scale = hd ** (-0.5)
     cells = 2 * ctx_n
@@ -98,20 +100,56 @@
             device_id={"ctx": c, "tp": z - 1}, device_id_type=MESH,
         )
 
-    def sends_right(s):
-        return jnp.logical_and(z - s >= 0, z + 1 < tp_n)
-
-    def sends_left(s):
-        return jnp.logical_and(z + s < tp_n, z - 1 >= 0)
+    def sends_right(s, i):
+        last = tp_n - 1 if i >= kept else tp_n
+        return jnp.logical_and(z - s >= 0, z + 1 < last)
+
+    def sends_left(s, i):
+        first = 1 if i >= kept else 0
+        return jnp.logical_and(z + s < tp_n, z - 1 >= first)
+
+    moved = moved_chunks(tp_n)
+    kept = CHUNKS - moved
+    proj = w_hbm.shape[0]
+    wr = proj // ctx_n
+    is_edge = jnp.logical_or(z == 0, z == tp_n - 1)
+    is_helper = jnp.logical_or(z == 1, z == tp_n - 2)
+    inward = jnp.where(z == 0, 1, -1)
+    beyond = jnp.where(z == 1, 1, -1)
+
+    def wx_rows(j):
+        return wx.at[:, pl.ds(pl.multiple_of(j * wr, wr), wr), :]
+
+    edge_copy = None
+    if moved:
+        edge_copy = pltpu.make_async_remote_copy(
+            src_ref=w.at[pl.ds(kept, moved), pl.ds(pl.multiple_of(c * wr, wr), wr), :],
+            dst_ref=wx_rows(c), send_sem=we_s, recv_sem=we_r,
+            device_id={"ctx": c, "tp": z + inward}, device_id_type=MESH,
+        )
+
+        @pl.when(is_edge)
+        def _():
+            for cp in w_copies:
+                cp.wait()
+            edge_copy.start()
+
+        @pl.when(jnp.logical_not(is_edge))
+        def _():
+            for cp in w_copies:
+                cp.wait()
+    else:
+        for cp in w_copies:
+            cp.wait()
 
     for i in range(CHUNKS):
         g_copies[i].wait()
 
-        @pl.when(sends_right(0))
+        @pl.when(sends_right(0, i))
         def _(i=i):
             right_copy(0, i).start()
 
-        @pl.when(sends_left(0))
+        @pl.when(sends_left(0, i))
         def _(i=i):
             left_copy(0, i).start()
 
@@ -122,7 +160,7 @@
         cp.start()
 
     down_pad[...] = jnp.zeros_like(down_pad)
-    down_pad[:, :rank] = down_ref[...]
+    down_pad[:rank, :] = down_ref[...]
     cot_own = jnp.zeros((blk, rank), F32)
     for i in range(CHUNKS):
         cot_own += dot(gath[z, i], up_ref[:, i * cw : (i + 1) * cw], NT)
@@ -131,7 +169,7 @@
     cot_copies = [tp_copy(k, cot.at[z], cot.at[z], cot_s, cot_r) for k in range(1, tp_n)]
     for cp in cot_copies:
         cp.start()
-    mix_send[...] = dot(ao_ref[...], down_pad[...]).reshape(mix_send.shape)
+    mix_send[...] = dot(ao_ref[...], down_pad[...], NT).reshape(mix_send.shape)
     mix_copies = [
         tp_copy(k, mix_send.at[lax.rem(z + k, tp_n)], mix_recv.at[z], mix_s, mix_r)
         for k in range(1, tp_n)
@@ -151,9 +189,6 @@
     dq_st[...] = jnp.zeros_like(dq_st)
     dkv_acc[...] = jnp.zeros_like(dkv_acc)
 
-    for cp in w_copies:
-        cp.wait()
-
     def project(b, i):
         dacc[b] += dot(gath[b, i], w[i], NT)
 
@@ -175,7 +210,18 @@
         for k in range(1, ctx_n)
     ]
     d_copies = [ctx_copy(k, d_recv.at[c], d_recv.at[c], d_s, d_r) for k in range(1, ctx_n)]
-    uz_copies = [tp_copy(k, uz.at[z], uz.at[z], uz_s, uz_r) for k in range(1, tp_n)]
+    rq = uz.shape[1]
+    scattered = rq < rank
+
+    def u_rows(t):
+        return u_sum.at[pl.ds(pl.multiple_of(t * rq, rq), rq), :] if scattered else u_sum
+
+    uz_copies = [
+        tp_copy(k, u_rows(lax.rem(z + k, tp_n)), uz.at[z], uz_s, uz_r) for k in range(1, tp_n)
+    ]
+    uc_copies = []
+    if scattered:
+        uc_copies = [tp_copy(k, uc.at[z], uc.at[z], uc_s, uc_r) for k in range(1, tp_n)]
     ua_copies = [ctx_copy(k, u_all.at[c], u_all.at[c], ua_s, ua_r) for k in range(1, ctx_n)]
 
     def first_parts():
@@ -227,9 +273,10 @@
         total = u_recv[0].astype(F32)
         for j in range(1, ctx_n):
             total += u_recv[j].astype(F32)
-        uz[z] = total.astype(BF16)
+        u_sum[...] = total.astype(BF16)
         for cp in uz_copies:
             cp.start()
+        uz[z] = u_rows(z)[...]
         for cp in d_copies:
             cp.wait_recv()
         total = d_recv[0].astype(F32)
@@ -243,19 +290,87 @@
         total = uz[0].astype(F32)
         for t in range(1, tp_n):
             total += uz[t].astype(F32)
-        u_all[c] = total.astype(BF16)
+        if scattered:
+            uc[z] = total.astype(BF16)
+            for cp in uc_copies:
+                cp.start()
+        else:
+            u_all[c] = total.astype(BF16)
+
+    def fourth_parts():
+        if scattered:
+            for cp in uc_copies:
+                cp.wait_recv()
+            u_all[c] = uc[...].reshape(u_all.shape[1:])
         for cp in ua_copies:
             cp.start()
+
+    sibling = c + 1 - 2 * lax.rem(c, 2)
+    own_rows = wx_rows(c) if moved else None
+    wa_copies, wf_copies = [], []
+    if moved:
+        wa_copies = [
+            ctx_copy(2 * k, own_rows, own_rows, wa_s, wa_r) for k in range(1, ctx_n // 2)
+        ]
+        for k in range(ctx_n // 2):
+            block = wx_rows(lax.rem(c + ctx_n - 2 * k, ctx_n))
+            wf_copies.append(
+                pltpu.make_async_remote_copy(
+                    src_ref=block, dst_ref=block, send_sem=wf_s.at[k], recv_sem=wf_r.at[k],
+                    device_id={"ctx": sibling, "tp": z}, device_id_type=MESH,
+                )
+            )
+
+    def px_copy(d):
+        return pltpu.make_async_remote_copy(
+            src_ref=px_send.at[d], dst_ref=px_recv.at[d], send_sem=px_s.at[d],
+            recv_sem=px_r.at[d], device_id={"ctx": c, "tp": z - beyond}, device_id_type=MESH,
+        )
+
+    def weight_in():
+        if moved:
+            @pl.when(is_helper)
+            def _():
+                edge_copy.wait_recv()
+                for cp in wa_copies:
+                    cp.start()
+                wf_copies[0].start()
+
+    def weight_on():
+        if moved:
+            @pl.when(is_helper)
+            def _():
+                for k in range(1, ctx_n // 2):
+                    wa_copies[k - 1].wait_recv()
+                    wf_copies[k].start()
+
+    def weight_whole():
+        if moved:
+            @pl.when(is_helper)
+            def _():
+                for cp in wf_copies:
+                    cp.wait_recv()
+
+    def help_with(d):
+        if moved and d <= tp_n - 2:
+            @pl.when(is_helper)
+            def _():
+                b = z + d * beyond
+                part = dot(gath[b, kept], wx[0], NT)
+                for i in range(1, moved):
+                    part += dot(gath[b, kept + i], wx[i], NT)
+                px_send[d] = part.astype(BF16)
+                px_copy(d).start()
 
     for s in range(tp_n - 1):
         from_left = z - 1 - s >= 0
         from_right = z + 1 + s < tp_n
         for i in range(CHUNKS):
-            @pl.when(from_left)
+            @pl.when(jnp.logical_and(from_left, z < (tp_n - 1 if i >= kept else tp_n)))
             def _(s=s, i=i):
                 right_copy(s, i).wait_recv()
 
-                @pl.when(z + 1 < tp_n)
+                @pl.when(z + 1 < (tp_n - 1 if i >= kept else tp_n))
                 def _():
                     pltpu.make_async_remote_copy(
                         src_ref=gath.at[z - 1 - s, i], dst_ref=gath.at[z - 1 - s, i],
@@ -265,11 +380,11 @@
 
                 project(z - 1 - s, i)
 
-            @pl.when(from_right)
+            @pl.when(jnp.logical_and(from_right, z > (0 if i >= kept else -1)))
             def _(s=s, i=i):
                 left_copy(s, i).wait_recv()
 
-                @pl.when(z - 1 >= 0)
+                @pl.when(z - 1 >= (1 if i >= kept else 0))
                 def _():
                     pltpu.make_async_remote_copy(
                         src_ref=gath.at[z + 1 + s, i], dst_ref=gath.at[z + 1 + s, i],
@@ -282,15 +397,37 @@
             if s == 0 and i == 0:
                 first_parts()
             if s == 0 and i == 2:
+                weight_in()
+            if s == 0 and i == 4:
                 probabilities()
             if s == 1 and i == 0:
+                weight_on()
                 second_parts()
             if s == 1 and i == 2:
                 third_parts()
+                weight_whole()
+                help_with(0)
+                help_with(1)
+            if s == 1 and i == 5:
+                fourth_parts()
+            if s >= 1 and i == CHUNKS - 1:
+                help_with(s + 1)
+
+    if moved:
+        @pl.when(is_edge)
+        def _():
+            for d in range(tp_n - 1):
+                b = z + (d + 1) * inward
+                pltpu.make_async_remote_copy(
+                    src_ref=px_send.at[d], dst_ref=px_recv.at[d], send_sem=px_s.at[d],
+                    recv_sem=px_r.at[d], device_id={"ctx": c, "tp": z + inward},
+                    device_id_type=MESH,
+                ).wait_recv()
+                dacc[b] += px_recv[d].astype(F32)
 
     cot_rows = cot[...].reshape(rows, cot.shape[2])
     d_attn = dacc[...].reshape(rows, dacc.shape[2]) + adapter_scale_factor * dot(
-        cot_rows, down_pad[...], NT
+        cot_rows, down_pad[...]
     )
     d_attn = d_attn.astype(BF16)
     for part in range(2):
@@ -356,20 +493,57 @@
     dv_out[...] = sums[1].astype(BF16)
 
     for group in (
-        kv_copies, cot_copies, mix_copies, ctx_up_copies, d_copies, uz_copies, ua_copies, dkv_copies
+        kv_copies, cot_copies, mix_copies, ctx_up_copies, d_copies, uz_copies, uc_copies,
+        ua_copies, dkv_copies,
     ):
         for cp in group:
             cp.wait_send()
     pair_copy.wait_send()
+    if moved:
+        @pl.when(is_edge)
+        def _():
+            edge_copy.wait_send()
+
+        @pl.when(is_helper)
+        def _():
+            for cp in wa_copies + wf_copies:
+                cp.wait_send()
+            for d in range(tp_n - 1):
+                px_copy(d).wait_send()
     for s in range(tp_n - 1):
         for i in range(CHUNKS):
-            @pl.when(sends_right(s))
+            @pl.when(sends_right(s, i))
             def _(s=s, i=i):
                 right_copy(s, i).wait_send()
 
-            @pl.when(sends_left(s))
+            @pl.when(sends_left(s, i))
             def _(s=s, i=i):
                 left_copy(s, i).wait_send()
+
+
+def moved_chunks(tp_n):
+    return MOVED if tp_n == 4 else 0
+
+
+def hand_on(*refs):
+    n = len(refs) // 2
+    sems = refs[-1]
+    copies = [pltpu.make_async_copy(refs[i], refs[n + i], sems.at[i]) for i in range(n)]
+    for cp in copies:
+        cp.start()
+    for cp in copies:
+        cp.wait()
+
+
+def handed_on(*arrays):
+    hbm = pl.BlockSpec(memory_space=pl.ANY)
+    return pl.pallas_call(
+        hand_on,
+        out_shape=tuple(jax.ShapeDtypeStruct(a.shape, a.dtype) for a in arrays),
+        in_specs=[hbm] * len(arrays),
+        out_specs=(hbm,) * len(arrays),
+        scratch_shapes=[pltpu.SemaphoreType.DMA((len(arrays),))],
+    )(*arrays)
 
 
 def local(q, k, v, ao, ln, g, w, down, up):
@@ -385,6 +559,8 @@
     uw = width // ctx_n
     proj = w.shape[0]
     rank = down.shape[1]
+    moves = moved_chunks(tp_n) > 0
+    rq = rank // tp_n if rank % (16 * tp_n) == 0 else rank
     lanes = max(128, rank)
     pairs = 2 * ctx_n + 1
     vmem = pl.BlockSpec(memory_space=pltpu.VMEM)
@@ -395,14 +571,19 @@
         V((tp_n, CHUNKS, blk, cw), BF16),
         V((CHUNKS, proj, cw), BF16),
         V((tp_n, blk, proj), F32),
-        V((proj, lanes), BF16),
+        V((lanes, proj), BF16),
         V((tp_n, blk, lanes), BF16),
         V((tp_n, blk, lanes), F32),
         V((tp_n, blk, lanes), F32),
         V((ctx_n, rank, uw), BF16),
         V((ctx_n, rank, uw), BF16),
-        V((tp_n, rank, uw), BF16),
+        V((rank, uw), BF16),
+        V((tp_n, rq, uw), BF16),
+        V((tp_n, rq, uw), BF16),
         V((ctx_n, rank, uw), BF16),
+        V((MOVED, proj, cw) if moves else (1, 16, 128), BF16),
+        V((tp_n, blk, proj) if moves else (1, 16, 128), BF16),
+        V((tp_n, blk, proj) if moves else (1, 16, 128), BF16),
         V((ctx_n, rank, proj), BF16),
         V((ctx_n, 2, rows, hd), BF16),
         V((pairs, half, heads * half), F32),
@@ -419,7 +600,8 @@
     ]
     scratch += [DMA((tp_n, CHUNKS))] * 4
     scratch += [DMA((ctx_n,))] * 2 + [DMA((tp_n,))] * 4 + [DMA((ctx_n,))] * 2
-    scratch += [DMA((tp_n,))] * 2 + [DMA((ctx_n,))] * 6 + [DMA, DMA]
+    scratch += [DMA((tp_n,))] * 4 + [DMA((ctx_n,))] * 6 + [DMA((tp_n,))] * 2
+    scratch += [DMA((ctx_n,))] * 4 + [DMA] * 4
     dq, dk, dv, dd, du = pl.pallas_call(
         functools.partial(kernel, ctx_n, tp_n, heads),
         out_shape=(
@@ -438,7 +620,8 @@
         cost_estimate=pl.CostEstimate(
             flops=5 * 10**9, bytes_accessed=16 * 2**20, transcendentals=2**21
         ),
-    )(q, k, v, ao, ln, g, w, down, up)
+    )(q, k, v, ao, ln, g, w, down.T, up)
+    dq, dk, dv, dd, du = handed_on(dq, dk, dv, dd, du)
     return dq, dk, dv, dd.T, du
 
 

time: 123 us -> 175 us (1.42)
  Pallas kernels: 112 us -> 173 us
  local copies, waits for them, and re-layouts: 10 us -> 0 us
    pallas_call x0 -> x1, Pallas kernels: none -> 48.8 us  [handed_on(): pl.pallas_call(hand_on, out_shape=tuple((jax.ShapeDtypeStruct(a.shape, a....]
    pallas_call x1, Pallas kernels: 112 us -> 124 us  [local(): pl.pallas_call(functools.partial(kernel, ctx_n, tp_n, heads), out_shape=(...]
    unnamed x6 -> x0, local copies, waits for them, and re-layouts: 10 us -> none
where the time goes in v2:
time: 175 us; the launch traced here: 174 us
  Pallas kernels  173 us (99%)
    pallas_call x1, Pallas kernels, local(): pl.pallas_call(functools.partial(kernel, ctx_n, tp_n, heads), out_shape=(...  124 us
    pallas_call x1, Pallas kernels, handed_on(): pl.pallas_call(hand_on, out_shape=tuple((jax.ShapeDtypeStruct(a.shape, a....  48.8 us

profile of v2, /device:TPU:0, one launch (start us, length us, event | category | flops | bytes accessed | tf_op | source)
XLA Modules:
  0.0 173.7 jit_solution(6631665771309836906)
XLA Ops:
  0.6 124.1 %shard_map.128 = (bf16[256,512]{1,0:T(8,128)(2,1)}, bf16[256,128]{1,0:T(8,128)(2,1)}, bf16[256,128]{1,0:T(8,128)(2,1)}, f32[64,512]{1,0:T(8,128)}, bf16[64,8192]{1,0:T(8,128)(2,1)}) custom-call(bf16[256,512]{1,0:T(8,128)(2,1)} %q_ref.1, bf16[256,128]{1,0:T(8,128)(2,1)} %k_ref.1, bf16[256,128]{1,0:T(8,128)(2,1)} %v_ref.1, bf16[256,512]{1,0:T(8,128)(2,1)} %ao_ref.1, ...), custom_call_target="tpu_custom_call" | custom-call | flops 5000000000 | bytes 16777216 | tf_op jit(solution)/shard_map/pallas_call | solution.py:605
  124.8 48.8 %shard_map.129 = (bf16[256,512]{1,0:T(8,128)(2,1)}, bf16[256,128]{1,0:T(8,128)(2,1)}, bf16[256,128]{1,0:T(8,128)(2,1)}, f32[64,512]{1,0:T(8,128)}, bf16[64,8192]{1,0:T(8,128)(2,1)}) custom-call(bf16[256,512]{1,0:T(8,128)(2,1)} %get-tuple-element.15.refs_0_, bf16[256,128]{1,0:T(8,128)(2,1)} %get-tuple-element.16.refs_1_, ...), custom_call_target="tpu_custom_call" | custom-call | tf_op jit(solution)/shard_map/pallas_call | solution.py:540

commit v3 on v2

--- a/solution.py
+++ b/solution.py
@@ -63,6 +63,10 @@
     for cp in w_copies:
         cp.start()
 
+    down_pad[...] = jnp.zeros_like(down_pad)
+    down_pad[:rank, :] = down_ref[...]
+    mix_send[...] = dot(ao_ref[...], down_pad[...], NT).reshape(mix_send.shape)
+
     barrier = pltpu.get_barrier_semaphore()
     for k in range(1, ctx_n):
         pl.semaphore_signal(
@@ -107,6 +111,14 @@
     def sends_left(s, i):
         first = 1 if i >= kept else 0
         return jnp.logical_and(z + s < tp_n, z - 1 >= first)
+
+    mix_copies = [
+        tp_copy(k, mix_send.at[lax.rem(z + k, tp_n)], mix_recv.at[z], mix_s, mix_r)
+        for k in range(1, tp_n)
+    ]
+    for cp in mix_copies:
+        cp.start()
+    mix_recv[z] = mix_send[z]
 
     moved = moved_chunks(tp_n)
     kept = CHUNKS - moved
@@ -128,20 +140,6 @@
             device_id={"ctx": c, "tp": z + inward}, device_id_type=MESH,
         )
 
-        @pl.when(is_edge)
-        def _():
-            for cp in w_copies:
-                cp.wait()
-            edge_copy.start()
-
-        @pl.when(jnp.logical_not(is_edge))
-        def _():
-            for cp in w_copies:
-                cp.wait()
-    else:
-        for cp in w_copies:
-            cp.wait()
-
     for i in range(CHUNKS):
         g_copies[i].wait()
 
@@ -152,6 +150,13 @@
         @pl.when(sends_left(0, i))
         def _(i=i):
             left_copy(0, i).start()
+
+    for cp in w_copies:
+        cp.wait()
+    if moved:
+        @pl.when(is_edge)
+        def _():
+            edge_copy.start()
 
     kv[c, 0] = k_ref[...]
     kv[c, 1] = v_ref[...]
@@ -159,8 +164,6 @@
     for cp in kv_copies:
         cp.start()
 
-    down_pad[...] = jnp.zeros_like(down_pad)
-    down_pad[:rank, :] = down_ref[...]
     cot_own = jnp.zeros((blk, rank), F32)
     for i in range(CHUNKS):
         cot_own += dot(gath[z, i], up_ref[:, i * cw : (i + 1) * cw], NT)
@@ -169,14 +172,6 @@
     cot_copies = [tp_copy(k, cot.at[z], cot.at[z], cot_s, cot_r) for k in range(1, tp_n)]
     for cp in cot_copies:
         cp.start()
-    mix_send[...] = dot(ao_ref[...], down_pad[...], NT).reshape(mix_send.shape)
-    mix_copies = [
-        tp_copy(k, mix_send.at[lax.rem(z + k, tp_n)], mix_recv.at[z], mix_s, mix_r)
-        for k in range(1, tp_n)
-    ]
-    for cp in mix_copies:
-        cp.start()
-    mix_recv[z] = mix_send[z]
 
     for part in range(2):
         for h in range(heads):
@@ -238,6 +233,8 @@
         for cp in ctx_up_copies:
             cp.start()
         u_recv[c] = u_send[c]
+
+    def down_parts():
         for cp in cot_copies:
             cp.wait_recv()
         cot_rows = cot[...].reshape(rows, cot.shape[2])
@@ -394,24 +391,27 @@
 
                 project(z + 1 + s, i)
 
-            if s == 0 and i == 0:
+            if s == 0 and i == 1:
                 first_parts()
-            if s == 0 and i == 2:
+            if s == 0 and i == 4:
+                down_parts()
+            if s == 1 and i == 0:
+                probabilities()
+            if s == 1 and i == 2:
                 weight_in()
-            if s == 0 and i == 4:
-                probabilities()
-            if s == 1 and i == 0:
+            if s == 1 and i == 4:
+                second_parts()
+            if s == 1 and i == 6:
+                third_parts()
+            if s == 1 and i == CHUNKS - 1:
                 weight_on()
-                second_parts()
-            if s == 1 and i == 2:
-                third_parts()
                 weight_whole()
-                help_with(0)
-                help_with(1)
-            if s == 1 and i == 5:
+                for d in range(min(3, tp_n - 1)):
+                    help_with(d)
+            if s >= 2 and i == CHUNKS - 1:
+                help_with(s + 1)
+            if s == 2 and i == 2:
                 fourth_parts()
-            if s >= 1 and i == CHUNKS - 1:
-                help_with(s + 1)
 
     if moved:
         @pl.when(is_edge)
@@ -527,22 +527,17 @@
 
 def hand_on(*refs):
     n = len(refs) // 2
-    sems = refs[-1]
-    copies = [pltpu.make_async_copy(refs[i], refs[n + i], sems.at[i]) for i in range(n)]
-    for cp in copies:
-        cp.start()
-    for cp in copies:
-        cp.wait()
+    for i in range(n):
+        refs[n + i][...] = refs[i][...]
 
 
 def handed_on(*arrays):
-    hbm = pl.BlockSpec(memory_space=pl.ANY)
+    vmem = pl.BlockSpec(memory_space=pltpu.VMEM)
     return pl.pallas_call(
         hand_on,
         out_shape=tuple(jax.ShapeDtypeStruct(a.shape, a.dtype) for a in arrays),
-        in_specs=[hbm] * len(arrays),
-        out_specs=(hbm,) * len(arrays),
-        scratch_shapes=[pltpu.SemaphoreType.DMA((len(arrays),))],
+        in_specs=[vmem] * len(arrays),
+        out_specs=(vmem,) * len(arrays),
     )(*arrays)
 
 

time: 175 us -> 109 us (0.62)
  Pallas kernels: 173 us -> 107 us
    pallas_call x1, Pallas kernels: 48.8 us -> 2.6 us  [handed_on(): pl.pallas_call(hand_on, out_shape=tuple((jax.ShapeDtypeStruct(a.shape, a....]
    pallas_call x1, Pallas kernels: 124 us -> 104 us  [local(): pl.pallas_call(functools.partial(kernel, ctx_n, tp_n, heads), out_shape=(...]
where the time goes in v3:
time: 109 us; the launch traced here: 107 us
  Pallas kernels  107 us (98%)
    pallas_call x1, Pallas kernels, local(): pl.pallas_call(functools.partial(kernel, ctx_n, tp_n, heads), out_shape=(...  104 us
    pallas_call x1, Pallas kernels, handed_on(): pl.pallas_call(hand_on, out_shape=tuple((jax.ShapeDtypeStruct(a.shape, a....  2.6 us

profile of v3, /device:TPU:0, one launch (start us, length us, event | category | flops | bytes accessed | tf_op | source)
XLA Modules:
  0.0 107.5 jit_solution(13804288405269166511)
XLA Ops:
  0.6 104.2 %shard_map.128 = (bf16[256,512]{1,0:T(8,128)(2,1)}, bf16[256,128]{1,0:T(8,128)(2,1)}, bf16[256,128]{1,0:T(8,128)(2,1)}, f32[64,512]{1,0:T(8,128)}, bf16[64,8192]{1,0:T(8,128)(2,1)}) custom-call(bf16[256,512]{1,0:T(8,128)(2,1)} %q_ref.1, bf16[256,128]{1,0:T(8,128)(2,1)} %k_ref.1, bf16[256,128]{1,0:T(8,128)(2,1)} %v_ref.1, bf16[256,512]{1,0:T(8,128)(2,1)} %ao_ref.1, ...), custom_call_target="tpu_custom_call" | custom-call | flops 5000000000 | bytes 16777216 | tf_op jit(solution)/shard_map/pallas_call | solution.py:600
  104.9 2.6 %shard_map.129 = (bf16[256,512]{1,0:T(8,128)(2,1)}, bf16[256,128]{1,0:T(8,128)(2,1)}, bf16[256,128]{1,0:T(8,128)(2,1)}, f32[64,512]{1,0:T(8,128)}, bf16[64,8192]{1,0:T(8,128)(2,1)}) custom-call(bf16[256,512]{1,0:T(8,128)(2,1)} %get-tuple-element.15.refs_0_, bf16[256,128]{1,0:T(8,128)(2,1)} %get-tuple-element.16.refs_1_, ...), custom_call_target="tpu_custom_call" | custom-call | tf_op jit(solution)/shard_map/pallas_call | solution.py:536

commit v4 on v3

--- a/solution.py
+++ b/solution.py
@@ -14,6 +14,7 @@
 NT = (((1,), (1,)), ((), ()))
 TN = (((0,), (0,)), ((), ()))
 CHUNKS = 8
+AHEAD = 3
 MOVED = 3
 KEPT = CHUNKS - MOVED
 
@@ -33,7 +34,7 @@
     dkv_acc, dkv_send, dkv_recv, pair_buf,
     loc_sem, gr_s, gr_r, gl_s, gl_r,
     kv_s, kv_r, cot_s, cot_r, mix_s, mix_r, u_s, u_r, uz_s, uz_r, uc_s, uc_r, ua_s, ua_r,
-    d_s, d_r, dkv_s, dkv_r, px_s, px_r, wa_s, wa_r, wf_s, wf_r, we_s, we_r, pair_s, pair_r,
+    d_s, d_r, dkv_s, dkv_r, px_s, px_r, wa_s, wa_r, half_s, half_r, we_s, we_r, pair_s, pair_r,
 ):
     c = lax.axis_index("ctx")
     z = lax.axis_index("tp")
@@ -140,28 +141,54 @@
             device_id={"ctx": c, "tp": z + inward}, device_id_type=MESH,
         )
 
+    def out_right(t, more=True):
+        s, i = divmod(t, CHUNKS)
+        if s < tp_n - 1:
+            @pl.when(jnp.logical_and(sends_right(s, i), more))
+            def _():
+                right_copy(s, i).start()
+
+    def out_left(t, more=True):
+        s, i = divmod(t, CHUNKS)
+        if s < tp_n - 1:
+            @pl.when(jnp.logical_and(sends_left(s, i), more))
+            def _():
+                left_copy(s, i).start()
+
     for i in range(CHUNKS):
         g_copies[i].wait()
-
-        @pl.when(sends_right(0, i))
-        def _(i=i):
-            right_copy(0, i).start()
-
-        @pl.when(sends_left(0, i))
-        def _(i=i):
-            left_copy(0, i).start()
+        if i < AHEAD:
+            out_right(i)
+            out_left(i)
 
     for cp in w_copies:
         cp.wait()
-    if moved:
-        @pl.when(is_edge)
-        def _():
-            edge_copy.start()
+    sibling = c + 1 - 2 * lax.rem(c, 2)
+    chips = ctx_n // 2
+
+    def sibling_copy(src, dst, s, r):
+        return pltpu.make_async_remote_copy(
+            src_ref=src, dst_ref=dst, send_sem=s, recv_sem=r,
+            device_id={"ctx": sibling, "tp": z}, device_id_type=MESH,
+        )
+
+    def shared_gather(at, s, r):
+        out = [ctx_copy(2 * k, at(c), at(c), s, r) for k in range(1, chips)]
+        on = []
+        for k in range(chips):
+            block = at(lax.rem(c + ctx_n - 2 * k, ctx_n))
+            on.append(sibling_copy(block, block, s.at[2 * k + 1], r.at[2 * k + 1]))
+        return out, on
+
+    def hand_over(out, on):
+        for k in range(1, chips):
+            out[k - 1].wait_recv()
+            on[k].start()
 
     kv[c, 0] = k_ref[...]
     kv[c, 1] = v_ref[...]
-    kv_copies = [ctx_copy(k, kv.at[c], kv.at[c], kv_s, kv_r) for k in range(1, ctx_n)]
-    for cp in kv_copies:
+    kv_out, kv_on = shared_gather(lambda j: kv.at[j], kv_s, kv_r)
+    for cp in kv_out + kv_on[:1]:
         cp.start()
 
     cot_own = jnp.zeros((blk, rank), F32)
@@ -188,8 +215,6 @@
         dacc[b] += dot(gath[b, i], w[i], NT)
 
     dacc[...] = jnp.zeros_like(dacc)
-    for i in range(CHUNKS):
-        project(z, i)
 
     def place(pair):
         early = pair <= c
@@ -217,7 +242,7 @@
     uc_copies = []
     if scattered:
         uc_copies = [tp_copy(k, uc.at[z], uc.at[z], uc_s, uc_r) for k in range(1, tp_n)]
-    ua_copies = [ctx_copy(k, u_all.at[c], u_all.at[c], ua_s, ua_r) for k in range(1, ctx_n)]
+    ua_out, ua_on = shared_gather(lambda j: u_all.at[j], ua_s, ua_r)
 
     def first_parts():
         for cp in mix_copies:
@@ -244,7 +269,7 @@
             cp.start()
 
     def probabilities():
-        for cp in kv_copies:
+        for cp in kv_on:
             cp.wait_recv()
 
         def body(pair, _):
@@ -299,24 +324,12 @@
             for cp in uc_copies:
                 cp.wait_recv()
             u_all[c] = uc[...].reshape(u_all.shape[1:])
-        for cp in ua_copies:
+        for cp in ua_out + ua_on[:1]:
             cp.start()
 
-    sibling = c + 1 - 2 * lax.rem(c, 2)
-    own_rows = wx_rows(c) if moved else None
     wa_copies, wf_copies = [], []
     if moved:
-        wa_copies = [
-            ctx_copy(2 * k, own_rows, own_rows, wa_s, wa_r) for k in range(1, ctx_n // 2)
-        ]
-        for k in range(ctx_n // 2):
-            block = wx_rows(lax.rem(c + ctx_n - 2 * k, ctx_n))
-            wf_copies.append(
-                pltpu.make_async_remote_copy(
-                    src_ref=block, dst_ref=block, send_sem=wf_s.at[k], recv_sem=wf_r.at[k],
-                    device_id={"ctx": sibling, "tp": z}, device_id_type=MESH,
-                )
-            )
+        wa_copies, wf_copies = shared_gather(wx_rows, wa_s, wa_r)
 
     def px_copy(d):
         return pltpu.make_async_remote_copy(
@@ -337,9 +350,7 @@
         if moved:
             @pl.when(is_helper)
             def _():
-                for k in range(1, ctx_n // 2):
-                    wa_copies[k - 1].wait_recv()
-                    wf_copies[k].start()
+                hand_over(wa_copies, wf_copies)
 
     def weight_whole():
         if moved:
@@ -359,42 +370,48 @@
                 px_send[d] = part.astype(BF16)
                 px_copy(d).start()
 
+    edge_right = jnp.logical_and(z + 1 == tp_n - 1, moved > 0)
+    edge_left = jnp.logical_and(z - 1 == 0, moved > 0)
     for s in range(tp_n - 1):
-        from_left = z - 1 - s >= 0
-        from_right = z + 1 + s < tp_n
         for i in range(CHUNKS):
-            @pl.when(jnp.logical_and(from_left, z < (tp_n - 1 if i >= kept else tp_n)))
+            got_left = jnp.logical_and(z - 1 - s >= 0, z < (tp_n - 1 if i >= kept else tp_n))
+            got_right = jnp.logical_and(z + 1 + s < tp_n, z > (0 if i >= kept else -1))
+
+            @pl.when(got_left)
             def _(s=s, i=i):
                 right_copy(s, i).wait_recv()
 
-                @pl.when(z + 1 < (tp_n - 1 if i >= kept else tp_n))
-                def _():
-                    pltpu.make_async_remote_copy(
-                        src_ref=gath.at[z - 1 - s, i], dst_ref=gath.at[z - 1 - s, i],
-                        send_sem=gr_s.at[s + 1, i], recv_sem=gr_r.at[s + 1, i],
-                        device_id={"ctx": c, "tp": z + 1}, device_id_type=MESH,
-                    ).start()
-
-                project(z - 1 - s, i)
-
-            @pl.when(jnp.logical_and(from_right, z > (0 if i >= kept else -1)))
+            @pl.when(got_right)
             def _(s=s, i=i):
                 left_copy(s, i).wait_recv()
 
-                @pl.when(z - 1 >= (1 if i >= kept else 0))
+            t = s * CHUNKS + i
+            first = t + AHEAD < CHUNKS
+            out_right(t + AHEAD, first or jnp.logical_not(edge_right))
+            out_left(t + AHEAD, first or jnp.logical_not(edge_left))
+            out_right(t + CHUNKS, edge_right)
+            out_left(t + CHUNKS, edge_left)
+            if moved and t == CHUNKS - AHEAD:
+                @pl.when(is_edge)
                 def _():
-                    pltpu.make_async_remote_copy(
-                        src_ref=gath.at[z + 1 + s, i], dst_ref=gath.at[z + 1 + s, i],
-                        send_sem=gl_s.at[s + 1, i], recv_sem=gl_r.at[s + 1, i],
-                        device_id={"ctx": c, "tp": z - 1}, device_id_type=MESH,
-                    ).start()
-
+                    edge_copy.start()
+            if s == 0:
+                project(z, i)
+
+            @pl.when(got_left)
+            def _(s=s, i=i):
+                project(z - 1 - s, i)
+
+            @pl.when(got_right)
+            def _(s=s, i=i):
                 project(z + 1 + s, i)
 
             if s == 0 and i == 1:
                 first_parts()
             if s == 0 and i == 4:
                 down_parts()
+            if s == 0 and i == 6:
+                hand_over(kv_out, kv_on)
             if s == 1 and i == 0:
                 probabilities()
             if s == 1 and i == 2:
@@ -453,33 +470,45 @@
 
     lax.fori_loop(0, cells + 1, backward, 0)
 
-    dkv_copies = [
-        ctx_copy(k, dkv_send.at[lax.rem(c + k, ctx_n)], dkv_recv.at[c], dkv_s, dkv_r)
-        for k in range(1, ctx_n)
-    ]
-    for k in list(range(1, ctx_n)):
-        j = lax.rem(c + k, ctx_n)
-        dkv_send[j, 0] = (dkv_acc[j, 0] * scale).astype(BF16)
-        dkv_send[j, 1] = dkv_acc[j, 1].astype(BF16)
-        dkv_copies[k - 1].start()
-    dkv_recv[c, 0] = (dkv_acc[c, 0] * scale).astype(BF16)
-    dkv_recv[c, 1] = dkv_acc[c, 1].astype(BF16)
+    side = lax.rem(c, 2)
+    chip = c // 2
+    half_copy = sibling_copy(dkv_send.at[1 - side], dkv_recv.at[0], half_s, half_r)
+    for m in range(chips):
+        dkv_send[1 - side, m, 0] = (dkv_acc[2 * m + 1 - side, 0] * scale).astype(BF16)
+        dkv_send[1 - side, m, 1] = dkv_acc[2 * m + 1 - side, 1].astype(BF16)
+    half_copy.start()
+    hand_over(ua_out, ua_on)
+    half_copy.wait_recv()
+    dkv_copies = []
+    for k in list(range(1, chips)) + [0]:
+        m = lax.rem(chip + k, chips)
+        for n, factor in ((0, scale), (1, 1.0)):
+            sums = dkv_acc[2 * m + side, n] * factor + dkv_recv[0, m, n].astype(F32)
+            if k:
+                dkv_send[side, m, n] = sums.astype(BF16)
+            else:
+                dkv_recv[1, m, n] = sums.astype(BF16)
+        if k:
+            dkv_copies.append(
+                ctx_copy(2 * k, dkv_send.at[side, m], dkv_recv.at[1, chip], dkv_s, dkv_r)
+            )
+            dkv_copies[-1].start()
 
     for part in range(2):
         for h in range(heads):
             dq_out[part * half : (part + 1) * half, h * hd : (h + 1) * hd] = (
                 dq_st[part, h * half : (h + 1) * half, :] * scale
             ).astype(BF16)
-    for cp in ua_copies:
+    for cp in ua_on:
         cp.wait_recv()
     for j in range(ctx_n):
         up_out[:, j * uw : (j + 1) * uw] = u_all[j]
 
     for cp in dkv_copies:
         cp.wait_recv()
-    total = dkv_recv[0].astype(F32)
-    for j in range(1, ctx_n):
-        total += dkv_recv[j].astype(F32)
+    total = dkv_recv[1, 0].astype(F32)
+    for m in range(1, chips):
+        total += dkv_recv[1, m].astype(F32)
     pair_buf[0] = total.astype(BF16)
     other = z + 1 - 2 * lax.rem(z, 2)
     pair_copy = pltpu.make_async_remote_copy(
@@ -493,8 +522,8 @@
     dv_out[...] = sums[1].astype(BF16)
 
     for group in (
-        kv_copies, cot_copies, mix_copies, ctx_up_copies, d_copies, uz_copies, uc_copies,
-        ua_copies, dkv_copies,
+        kv_out, kv_on, cot_copies, mix_copies, ctx_up_copies, d_copies, uz_copies, uc_copies,
+        ua_out, ua_on, [half_copy], dkv_copies,
     ):
         for cp in group:
             cp.wait_send()
@@ -588,15 +617,15 @@
         V((2, 1, heads * half), F32),
         V((2, heads * half, hd), F32),
         V((ctx_n, 2, rows, hd), F32),
-        V((ctx_n, 2, rows, hd), BF16),
-        V((ctx_n, 2, rows, hd), BF16),
+        V((2, ctx_n // 2, 2, rows, hd), BF16),
+        V((2, ctx_n // 2, 2, rows, hd), BF16),
         V((2, 2, rows, hd), BF16),
         DMA((2 * CHUNKS,)),
     ]
     scratch += [DMA((tp_n, CHUNKS))] * 4
     scratch += [DMA((ctx_n,))] * 2 + [DMA((tp_n,))] * 4 + [DMA((ctx_n,))] * 2
     scratch += [DMA((tp_n,))] * 4 + [DMA((ctx_n,))] * 6 + [DMA((tp_n,))] * 2
-    scratch += [DMA((ctx_n,))] * 4 + [DMA] * 4
+    scratch += [DMA((ctx_n,))] * 2 + [DMA] * 6
     dq, dk, dv, dd, du = pl.pallas_call(
         functools.partial(kernel, ctx_n, tp_n, heads),
         out_shape=(

time: 109 us -> 98.9 us (0.907)
  Pallas kernels: 107 us -> 97.8 us
    pallas_call x1, Pallas kernels: 104 us -> 95.2 us  [local(): pl.pallas_call(functools.partial(kernel, ctx_n, tp_n, heads), out_shape=(...]
where the time goes in v4:
time: 98.9 us; the launch traced here: 98.5 us
  Pallas kernels  97.8 us (99%)
    pallas_call x1, Pallas kernels, local(): pl.pallas_call(functools.partial(kernel, ctx_n, tp_n, heads), out_shape=(...  95.2 us
    pallas_call x1, Pallas kernels, handed_on(): pl.pallas_call(hand_on, out_shape=tuple((jax.ShapeDtypeStruct(a.shape, a....  2.6 us

profile of v4, /device:TPU:0, one launch (start us, length us, event | category | flops | bytes accessed | tf_op | source)
XLA Modules:
  0.0 98.5 jit_solution(2259728842402714975)
XLA Ops:
  0.6 95.2 %shard_map.128 = (bf16[256,512]{1,0:T(8,128)(2,1)}, bf16[256,128]{1,0:T(8,128)(2,1)}, bf16[256,128]{1,0:T(8,128)(2,1)}, f32[64,512]{1,0:T(8,128)}, bf16[64,8192]{1,0:T(8,128)(2,1)}) custom-call(bf16[256,512]{1,0:T(8,128)(2,1)} %q_ref.1, bf16[256,128]{1,0:T(8,128)(2,1)} %k_ref.1, bf16[256,128]{1,0:T(8,128)(2,1)} %v_ref.1, bf16[256,512]{1,0:T(8,128)(2,1)} %ao_ref.1, ...), custom_call_target="tpu_custom_call" | custom-call | flops 5000000000 | bytes 16777216 | tf_op jit(solution)/shard_map/pallas_call | solution.py:629
  95.9 2.6 %shard_map.129 = (bf16[256,512]{1,0:T(8,128)(2,1)}, bf16[256,128]{1,0:T(8,128)(2,1)}, bf16[256,128]{1,0:T(8,128)(2,1)}, f32[64,512]{1,0:T(8,128)}, bf16[64,8192]{1,0:T(8,128)(2,1)}) custom-call(bf16[256,512]{1,0:T(8,128)(2,1)} %get-tuple-element.15.refs_0_, bf16[256,128]{1,0:T(8,128)(2,1)} %get-tuple-element.16.refs_1_, ...), custom_call_target="tpu_custom_call" | custom-call | tf_op jit(solution)/shard_map/pallas_call | solution.py:565

commit v5 on v4

--- a/solution.py
+++ b/solution.py
@@ -15,7 +15,7 @@
 TN = (((0,), (0,)), ((), ()))
 CHUNKS = 8
 AHEAD = 3
-MOVED = 3
+MOVED = 2
 KEPT = CHUNKS - MOVED
 
 
@@ -331,10 +331,13 @@
     if moved:
         wa_copies, wf_copies = shared_gather(wx_rows, wa_s, wa_r)
 
-    def px_copy(d):
-        return pltpu.make_async_remote_copy(
-            src_ref=px_send.at[d], dst_ref=px_recv.at[d], send_sem=px_s.at[d],
-            recv_sem=px_r.at[d], device_id={"ctx": c, "tp": z - beyond}, device_id_type=MESH,
+    others = pl.ds(0, tp_n - 1)
+    px_base = jnp.where(z < tp_n // 2, 1, 0)
+    px_copy = None
+    if moved:
+        px_copy = pltpu.make_async_remote_copy(
+            src_ref=px_send.at[others], dst_ref=px_recv.at[others], send_sem=px_s.at[0],
+            recv_sem=px_r.at[0], device_id={"ctx": c, "tp": z - beyond}, device_id_type=MESH,
         )
 
     def weight_in():
@@ -359,16 +362,16 @@
                 for cp in wf_copies:
                     cp.wait_recv()
 
-    def help_with(d):
-        if moved and d <= tp_n - 2:
+    def help_out():
+        if moved:
             @pl.when(is_helper)
             def _():
-                b = z + d * beyond
-                part = dot(gath[b, kept], wx[0], NT)
-                for i in range(1, moved):
-                    part += dot(gath[b, kept + i], wx[i], NT)
-                px_send[d] = part.astype(BF16)
-                px_copy(d).start()
+                part = jnp.zeros(((tp_n - 1) * blk, proj), F32)
+                for i in range(moved):
+                    g_rows = gath[pl.ds(px_base, tp_n - 1), kept + i]
+                    part += dot(g_rows.reshape((tp_n - 1) * blk, cw), wx[i], NT)
+                px_send[: tp_n - 1] = part.astype(BF16).reshape(tp_n - 1, blk, proj)
+                px_copy.start()
 
     edge_right = jnp.logical_and(z + 1 == tp_n - 1, moved > 0)
     edge_left = jnp.logical_and(z - 1 == 0, moved > 0)
@@ -423,24 +426,15 @@
             if s == 1 and i == CHUNKS - 1:
                 weight_on()
                 weight_whole()
-                for d in range(min(3, tp_n - 1)):
-                    help_with(d)
-            if s >= 2 and i == CHUNKS - 1:
-                help_with(s + 1)
+                help_out()
             if s == 2 and i == 2:
                 fourth_parts()
 
     if moved:
         @pl.when(is_edge)
         def _():
-            for d in range(tp_n - 1):
-                b = z + (d + 1) * inward
-                pltpu.make_async_remote_copy(
-                    src_ref=px_send.at[d], dst_ref=px_recv.at[d], send_sem=px_s.at[d],
-                    recv_sem=px_r.at[d], device_id={"ctx": c, "tp": z + inward},
-                    device_id_type=MESH,
-                ).wait_recv()
-                dacc[b] += px_recv[d].astype(F32)
+            px_copy.wait_recv()
+            dacc[pl.ds(px_base, tp_n - 1)] += px_recv[: tp_n - 1].astype(F32)
 
     cot_rows = cot[...].reshape(rows, cot.shape[2])
     d_attn = dacc[...].reshape(rows, dacc.shape[2]) + adapter_scale_factor * dot(
@@ -468,7 +462,7 @@
         dq_st[part] += dot(score_grad, keys, TN)
         return 0
 
-    lax.fori_loop(0, cells + 1, backward, 0)
+    lax.fori_loop(0, cells + 1, backward, 0, unroll=True)
 
     side = lax.rem(c, 2)
     chip = c // 2
@@ -537,8 +531,7 @@
         def _():
             for cp in wa_copies + wf_copies:
                 cp.wait_send()
-            for d in range(tp_n - 1):
-                px_copy(d).wait_send()
+            px_copy.wait_send()
     for s in range(tp_n - 1):
         for i in range(CHUNKS):
             @pl.when(sends_right(s, i))

time: 98.9 us -> 94.3 us (0.953)
  Pallas kernels: 97.8 us -> 93.5 us
    pallas_call x1, Pallas kernels: 95.2 us -> 90.9 us  [local(): pl.pallas_call(functools.partial(kernel, ctx_n, tp_n, heads), out_shape=(...]
where the time goes in v5:
time: 94.3 us; the launch traced here: 94.2 us
  Pallas kernels  93.5 us (99%)
    pallas_call x1, Pallas kernels, local(): pl.pallas_call(functools.partial(kernel, ctx_n, tp_n, heads), out_shape=(...  90.9 us
    pallas_call x1, Pallas kernels, handed_on(): pl.pallas_call(hand_on, out_shape=tuple((jax.ShapeDtypeStruct(a.shape, a....  2.6 us

profile of v5, /device:TPU:0, one launch (start us, length us, event | category | flops | bytes accessed | tf_op | source)
XLA Modules:
  0.0 94.2 jit_solution(10742147318094855376)
XLA Ops:
  0.6 90.9 %shard_map.128 = (bf16[256,512]{1,0:T(8,128)(2,1)}, bf16[256,128]{1,0:T(8,128)(2,1)}, bf16[256,128]{1,0:T(8,128)(2,1)}, f32[64,512]{1,0:T(8,128)}, bf16[64,8192]{1,0:T(8,128)(2,1)}) custom-call(bf16[256,512]{1,0:T(8,128)(2,1)} %q_ref.1, bf16[256,128]{1,0:T(8,128)(2,1)} %k_ref.1, bf16[256,128]{1,0:T(8,128)(2,1)} %v_ref.1, bf16[256,512]{1,0:T(8,128)(2,1)} %ao_ref.1, ...), custom_call_target="tpu_custom_call" | custom-call | flops 5000000000 | bytes 16777216 | tf_op jit(solution)/shard_map/pallas_call | solution.py:622
  91.6 2.6 %shard_map.129 = (bf16[256,512]{1,0:T(8,128)(2,1)}, bf16[256,128]{1,0:T(8,128)(2,1)}, bf16[256,128]{1,0:T(8,128)(2,1)}, f32[64,512]{1,0:T(8,128)}, bf16[64,8192]{1,0:T(8,128)(2,1)}) custom-call(bf16[256,512]{1,0:T(8,128)(2,1)} %get-tuple-element.15.refs_0_, bf16[256,128]{1,0:T(8,128)(2,1)} %get-tuple-element.16.refs_1_, ...), custom_call_target="tpu_custom_call" | custom-call | tf_op jit(solution)/shard_map/pallas_call | solution.py:558

commit v6 on v5

--- a/solution.py
+++ b/solution.py
@@ -394,7 +394,7 @@
             out_left(t + AHEAD, first or jnp.logical_not(edge_left))
             out_right(t + CHUNKS, edge_right)
             out_left(t + CHUNKS, edge_left)
-            if moved and t == CHUNKS - AHEAD:
+            if moved and t == 2:
                 @pl.when(is_edge)
                 def _():
                     edge_copy.start()

time: 94.3 us -> 93.5 us (level)
  Pallas kernels: 93.5 us -> 92.2 us
    pallas_call x1, Pallas kernels: 90.9 us -> 89.6 us  [local(): pl.pallas_call(functools.partial(kernel, ctx_n, tp_n, heads), out_shape=(...]
where the time goes in v6:
time: 93.5 us; the launch traced here: 92.8 us
  Pallas kernels  92.2 us (99%)
    pallas_call x1, Pallas kernels, local(): pl.pallas_call(functools.partial(kernel, ctx_n, tp_n, heads), out_shape=(...  89.6 us
    pallas_call x1, Pallas kernels, handed_on(): pl.pallas_call(hand_on, out_shape=tuple((jax.ShapeDtypeStruct(a.shape, a....  2.6 us

profile of v6, /device:TPU:0, one launch (start us, length us, event | category | flops | bytes accessed | tf_op | source)
XLA Modules:
  0.0 92.8 jit_solution(1866303470405953389)
XLA Ops:
  0.6 89.6 %shard_map.128 = (bf16[256,512]{1,0:T(8,128)(2,1)}, bf16[256,128]{1,0:T(8,128)(2,1)}, bf16[256,128]{1,0:T(8,128)(2,1)}, f32[64,512]{1,0:T(8,128)}, bf16[64,8192]{1,0:T(8,128)(2,1)}) custom-call(bf16[256,512]{1,0:T(8,128)(2,1)} %q_ref.1, bf16[256,128]{1,0:T(8,128)(2,1)} %k_ref.1, bf16[256,128]{1,0:T(8,128)(2,1)} %v_ref.1, bf16[256,512]{1,0:T(8,128)(2,1)} %ao_ref.1, ...), custom_call_target="tpu_custom_call" | custom-call | flops 5000000000 | bytes 16777216 | tf_op jit(solution)/shard_map/pallas_call | solution.py:622
  90.2 2.6 %shard_map.129 = (bf16[256,512]{1,0:T(8,128)(2,1)}, bf16[256,128]{1,0:T(8,128)(2,1)}, bf16[256,128]{1,0:T(8,128)(2,1)}, f32[64,512]{1,0:T(8,128)}, bf16[64,8192]{1,0:T(8,128)(2,1)}) custom-call(bf16[256,512]{1,0:T(8,128)(2,1)} %get-tuple-element.15.refs_0_, bf16[256,128]{1,0:T(8,128)(2,1)} %get-tuple-element.16.refs_1_, ...), custom_call_target="tpu_custom_call" | custom-call | tf_op jit(solution)/shard_map/pallas_call | solution.py:558
